TPU v7x, 32 devices: a whole 2x2x4 slice. The times are simulated.
32 devices in a mesh: lat: 8 (over z, x), lev: 4 (over y, core).
Axes of the slice: x: 2, y: 2, z: 4, core: 2. Of those that a mesh axis runs over, the one named last changes fastest.
Arguments:
- thickness: float32 [8, 128, 1440], P('lev', 'lat'), may hold values from 0.5 to 1.5
- tracers: float32 [8, 8, 128, 1440], P(None, 'lev', 'lat'), may hold values from 0 to 1
- east_courant: float32 [8, 128, 1440], P('lev', 'lat'), may hold values from -1.75 to 1.75
- north_courant: float32 [8, 128, 1440], P('lev', 'lat'), may hold values from -1.75 to 1.75
- vert_courant: float32 [8, 128, 1440], P('lev', 'lat'), may hold values from -1.75 to 1.75
- filter_flags: int32 [128], replicated, may hold values from 0 to 1, as said below
- owner_slots: int32 [128], replicated, may hold values from -1 to 71, as said below
Outputs:
- new_thickness: float32 [8, 128, 1440], P('lev', 'lat')
- new_tracer_mass: float32 [8, 8, 128, 1440], P(None, 'lev', 'lat')
- slot_spectra: float32 [72, 8, 1440], P('lat', 'lev')
Inputs may be any that keep to these rules, and one draw needn't show every extreme that they name: `filter_flags`: exactly 72 rows are 1, among them the first 16 and the last 16 rows. `owner_slots`: -1 on rows with flag 0; the flagged rows hold distinct slots covering 0 to 71; slot s is owned by lat index s // 9; the flagged rows of one lat index have at most 2 slots with one owner, and some lat index has exactly 2 with some owner.
All inputs are finite; a program needn't handle non-finite values.
Results may differ from a plain program's by a relative error of at most 0.000076.
Values sent between devices are 32-bit elements; how exact they have to be, the bound alone decides.
A program may use at most 128 MiB of HBM per device.

v0:
```python
import math

import jax
import jax.numpy as jnp
from jax import lax
from jax.sharding import PartitionSpec as P

SLOT_DEV = 9


PI = math.pi
COS_CUT = math.cos(40.0 * math.pi / 180.0)


def padded_2(cells, sides, width):
    for axis, dim in sides:
        count = lax.axis_size(axis)
        ends = count - 1
        head = lax.slice_in_dim(cells, 0, width, axis=dim)
        tail = lax.slice_in_dim(cells, cells.shape[dim] - width, cells.shape[dim], axis=dim)
        cells = jnp.concatenate(
            [
                lax.ppermute(tail, axis, [(i, (i + 1) % count) for i in range(ends)]),
                cells,
                lax.ppermute(head, axis, [((i + 1) % count, i) for i in range(ends)]),
            ],
            axis=dim,
        )
    return cells


def spectral_table(nlon):
    column_ids = jnp.arange(nlon, dtype=jnp.int32)
    nyquist = nlon // 2
    wave_num = jnp.where(column_ids <= nyquist, column_ids, column_ids - nyquist)
    angles = (column_ids[:, None] * wave_num[None, :] % nlon).astype(jnp.float32) * (
        2.0 * PI / nlon
    )
    weights = jnp.where(
        (column_ids == 0) | (column_ids == nyquist), math.sqrt(1.0 / nlon), math.sqrt(2.0 / nlon)
    ).astype(jnp.float32)
    return (
        jnp.where(column_ids[None, :] <= nyquist, jnp.cos(angles), jnp.sin(angles))
        * weights[None, :]
    )


def damping(cos_ratio, nlon):
    column_ids = jnp.arange(nlon, dtype=jnp.int32)
    nyquist = nlon // 2
    wave_num = jnp.where(column_ids <= nyquist, column_ids, column_ids - nyquist)
    sine_wave = jnp.abs(jnp.sin(wave_num.astype(jnp.float32) * (PI / nlon)))
    fraction = cos_ratio[:, None] / jnp.maximum(cos_ratio[:, None], sine_wave[None, :])
    return fraction * fraction


def cell_cosine(row_ids, total_rows):
    return jnp.cos((row_ids.astype(jnp.float32) + 0.5) * (PI / total_rows) - 0.5 * PI)


def face_cosine(row_ids, total_rows):
    return jnp.sin((row_ids + 1).astype(jnp.float32) * (PI / total_rows)) * (
        row_ids + 1 < total_rows
    ).astype(jnp.float32)


def upwind(courant, first, second):
    return jnp.maximum(courant, 0.0) * first + jnp.minimum(courant, 0.0) * second


def local(thickness, tracers, east_courant, north_courant, vert_courant, filter_flags, owner_slots):
    highest = lax.Precision.HIGHEST
    lev_dev, lat_dev, nlon = thickness.shape
    lat_count = lax.axis_size("lat")
    lev_count = lax.axis_size("lev")
    my_band = lax.axis_index("lat")
    my_levels = lax.axis_index("lev")
    total_rows = lat_dev * lat_count
    total_levels = lev_dev * lev_count
    fields_all = jnp.concatenate([thickness[None], thickness[None] * tracers], axis=0)
    field_count = fields_all.shape[0]
    stacked = jnp.concatenate([fields_all, north_courant[None], vert_courant[None]], axis=0)
    padded = padded_2(stacked, (("lat", 2), ("lev", 1)), 1)
    x_north = padded[:field_count, 1:-1, 2:]
    x_south = padded[:field_count, 1:-1, :-2]
    south_courant = padded[field_count, 1:-1, :-2]
    x_below = padded[:field_count, 2:, 1:-1]
    x_above = padded[:field_count, :-2, 1:-1]
    above_courant = padded[field_count + 1, :-2, 1:-1]
    row_ids = my_band * lat_dev + jnp.arange(lat_dev, dtype=jnp.int32)
    level_ids = my_levels * lev_dev + jnp.arange(lev_dev, dtype=jnp.int32)
    east_flux = upwind(east_courant, fields_all, jnp.roll(fields_all, -1, axis=3))
    div_east = east_flux - jnp.roll(east_flux, 1, axis=3)
    north_flux = (
        upwind(north_courant, fields_all, x_north) * face_cosine(row_ids, total_rows)[:, None]
    )
    north_prev = (
        upwind(south_courant, x_south, fields_all) * face_cosine(row_ids - 1, total_rows)[:, None]
    )
    div_north = (north_flux - north_prev) / cell_cosine(row_ids, total_rows)[:, None]
    vert_flux = (
        upwind(vert_courant, fields_all, x_below)
        * (level_ids + 1 < total_levels).astype(jnp.float32)[:, None, None]
    )
    vert_prev = (
        upwind(above_courant, x_above, fields_all)
        * (level_ids < total_levels).astype(jnp.float32)[:, None, None]
    )
    div_vert = vert_flux - vert_prev
    change = -(div_east + div_north + div_vert)
    flagged = filter_flags == 1
    owner_all = jnp.where(flagged, owner_slots // SLOT_DEV, -1)
    place_all = jnp.where(flagged, owner_slots % SLOT_DEV, 0)
    all_rows = jnp.arange(total_rows, dtype=jnp.int32)
    source_all = all_rows // lat_dev
    earlier = (
        (source_all[:, None] == source_all[None, :])
        & (owner_all[:, None] == owner_all[None, :])
        & (all_rows[None, :] < all_rows[:, None])
    )
    rank_all = jnp.sum(earlier.astype(jnp.int32), axis=1)
    slot_cap = -(-lat_dev // lat_count)
    buffer_rows = lat_count * slot_cap
    buffer_ids = jnp.arange(buffer_rows, dtype=jnp.int32)
    key_all = jnp.where(flagged, owner_all * slot_cap + rank_all, -1)
    local_key = lax.dynamic_slice_in_dim(key_all, my_band * lat_dev, lat_dev)
    local_flag = lax.dynamic_slice_in_dim(filter_flags, my_band * lat_dev, lat_dev) == 1
    pack_map = (buffer_ids[:, None] == local_key[None, :]).astype(jnp.float32)
    mine = flagged & (owner_all == my_band)
    place_map = (
        (jnp.arange(SLOT_DEV, dtype=jnp.int32)[:, None] == place_all[None, :]) & mine[None, :]
    ).astype(jnp.float32)
    arrive_map = ((source_all * slot_cap + rank_all)[:, None] == buffer_ids[None, :]).astype(
        jnp.float32
    )
    collect_map = jnp.dot(place_map, arrive_map, precision=highest)
    dft_table = spectral_table(nlon)
    slot_ratio = jnp.dot(place_map, cell_cosine(all_rows, total_rows) / COS_CUT, precision=highest)
    outgoing = jnp.einsum("ql,fkli->qfki", pack_map, change, precision=highest).reshape(
        lat_count, slot_cap, field_count, lev_dev, nlon
    )
    arrived = lax.all_to_all(outgoing, "lat", split_axis=0, concat_axis=0, tiled=True).reshape(
        buffer_rows, field_count, lev_dev, nlon
    )
    slot_data = jnp.einsum("pq,qfki->pfki", collect_map, arrived, precision=highest)
    coeffs = (
        jnp.einsum("pfki,ic->pfkc", slot_data, dft_table, precision=highest)
        * damping(slot_ratio, nlon)[:, None, None, :]
    )
    spectra = coeffs[:, 0]
    restored = jnp.einsum("pfkc,ic->pfki", coeffs, dft_table, precision=highest)
    returning = jnp.einsum("pq,pfki->qfki", collect_map, restored, precision=highest).reshape(
        lat_count, slot_cap, field_count, lev_dev, nlon
    )
    came_back = lax.all_to_all(returning, "lat", split_axis=0, concat_axis=0, tiled=True).reshape(
        buffer_rows, field_count, lev_dev, nlon
    )
    unpacked = jnp.einsum("ql,qfki->fkli", pack_map, came_back, precision=highest)
    change = jnp.where(local_flag[None, None, :, None], unpacked, change)
    updated = fields_all + change
    return (updated[0], updated[1:], spectra)


def solution(mesh):
    return jax.shard_map(
        local,
        mesh=mesh,
        in_specs=(
            P("lev", "lat", None),
            P(None, "lev", "lat", None),
            P("lev", "lat", None),
            P("lev", "lat", None),
            P("lev", "lat", None),
            P(),
            P(),
        ),
        out_specs=(P("lev", "lat", None), P(None, "lev", "lat", None), P("lat", "lev", None)),
        check_vma=False,
    )
```

profile of v0, /device:TPU:1, one launch (start us, length us, event | category | flops | bytes accessed | tf_op | source)
XLA Modules:
  0.0 230.5 jit_solution(6582023923383074641)
XLA Ops:
  4.5 5.2 %collective-permute-start.1 = (f32[11,2,1,1440]{3,2,1,0:T(1,128)}, f32[11,2,1,1440]{3,2,1,0:T(1,128)}, u32[]{:S(2)}, u32[]{:S(2)}) collective-permute-start(f32[11,2,1,1440]{3,2,1,0:T(1,128)} %get-tuple-element.13), channel_id=1, source_target_pairs={{0,4},{4,8},{8,12},{12,16},{16,20},{20,24},{24,28},{1,5},{5,9},{9,... | collective-permute-start | bytes 380168 | tf_op jit(solution)/shard_map/ppermute | solution.py:23
  9.7 1.8 fusion.26
  16.1 2.0 fusion.45
  21.0 1.7 pad_maximum_fusion
  24.2 4.5 %collective-permute-start.3 = (f32[11,1,18,1440]{3,1,2,0:T(1,128)S(1)}, f32[11,1,18,1440]{3,1,2,0:T(1,128)S(1)}, u32[]{:S(2)}, u32[]{:S(2)}) collective-permute-start(f32[11,1,18,1440]{3,1,2,0:T(1,128)S(1)} %copy.36), channel_id=1, source_target_pairs={{0,1},{1,2},{2,3},{4,5},{5,6},{6,7},{8,9},{9,10},{10,11},{12,13},{... | collective-permute-start | bytes 3421448 | tf_op jit(solution)/shard_map/ppermute | solution.py:23
  31.0 1.9 collective-permute-start.2
  33.7 8.6 %collective-permute-done.3 = f32[11,1,18,1440]{3,1,2,0:T(1,128)S(1)} collective-permute-done((f32[11,1,18,1440]{3,1,2,0:T(1,128)S(1)}, f32[11,1,18,1440]{3,1,2,0:T(1,128)S(1)}, u32[]{:S(2)}, u32[]{:S(2)}) %collective-permute-start.3) | collective-permute-done | bytes 1140512 | tf_op jit(solution)/shard_map/ppermute | solution.py:23
  43.3 5.6 %collective-permute-done.2 = f32[11,1,18,1440]{3,1,2,0:T(1,128)S(1)} collective-permute-done((f32[11,1,18,1440]{3,1,2,0:T(1,128)S(1)}, f32[11,1,18,1440]{3,1,2,0:T(1,128)S(1)}, u32[]{:S(2)}, u32[]{:S(2)}) %collective-permute-start.2) | collective-permute-done | bytes 1140512 | tf_op jit(solution)/shard_map/ppermute | solution.py:25
  49.1 4.1 %fusion.32 = f32[9,2,16,1440]{3,2,1,0:T(8,128)S(1)} fusion(f32[11,1,18,1440]{3,2,1,0:T(8,128)S(1)} %copy.37, f32[11,2,1,1440]{3,2,1,0:T(1,128)} %collective-permute-done, f32[11,2,1,1440]{3,2,1,0:T(1,128)} %collective-permute-done.1, f32[1,2,16,1440]{3,2,1,0:T(8,128)S(1)} %bitcast.88, f32[1,2,16,1440]{3,2,1,0:T(8,128)S(1)} %bitcast.92, ...), kind=kLoop, calls=%fused_computation.39 | loop fusion | flops 18662400 | bytes 11013328 | tf_op jit(solution)/shard_map/neg | solution.py:110
  54.4 2.3 fusion.58
  56.6 2.4 %reshape.160 = f32[8,2,9,2,1440]{4,1,0,3,2:T(2,128)S(1)} reshape(f32[16,9,2,1440]{3,0,2,1:T(8,128)} %fusion.58) | data formatting | bytes 3317760 | tf_op jit(solution)/shard_map/reshape | solution.py:139
  59.0 1.9 copy.39
  60.9 5.1 %all-to-all-start = ((f32[8,2,9,2,1440]{4,1,3,2,0:T(2,128)}), f32[8,2,9,2,1440]{4,1,3,2,0:T(2,128)S(1)}, u32[]{:S(2)}, u32[]{:S(2)}) async-start(f32[8,2,9,2,1440]{4,1,3,2,0:T(2,128)} %copy.39), calls=%async_computation | async-start | bytes 3538944 | tf_op jit(solution)/shard_map/all_to_all | solution.py:142
  66.0 39.1 %fusion.106 = f32[1440,1440,1,1]{1,0,3,2:T(8,128)} fusion(f32[1440]{0:T(1024)S(1)} %fusion.61, s32[1440]{0:T(1024)S(1)} %add_select_fusion.1, pred[1440]{0:T(1024)(128)(4,1)} %iota_compare_fusion.5), kind=kLoop, calls=%fused_computation.6.clone.clone.clone.1 | loop fusion | flops 22809600 | bytes 8307360 | tf_op jit(solution)/shard_map/pfki,ic->pfkc/dot_general | solution.py:147
  105.1 38.3 %fusion.104 = f32[1440,1440,1,1]{1,0,3,2:T(8,128)} fusion(f32[1440]{0:T(1024)S(1)} %fusion.61, s32[1440]{0:T(1024)S(1)} %add_select_fusion.1, pred[1440]{0:T(1024)(128)(4,1)S(1)} %copy-done.12), kind=kLoop, calls=%fused_computation.4.clone.1 | loop fusion | flops 22809600 | bytes 8307360 | tf_op jit(solution)/shard_map/pfkc,ic->pfki/dot_general | solution.py:151
  146.1 21.3 %fusion.21 = f32[9,9,2,1440]{3,1,2,0:T(8,128)S(1)} fusion(f32[9,9,2,1440]{3,0,2,1:T(8,128)S(1)} %fusion.48, f32[9,1440]{1,0:T(8,128)S(1)} %copy-done.9, f32[1440,1440,1,1]{1,0,3,2:T(8,128)} %fusion.106), kind=kOutput, calls=%fused_computation.28 | convolution fusion | flops 4031311616 | bytes 10212480 | tf_op jit(solution)/shard_map/pfki,ic->pfkc/dot_general | solution.py:147
  167.4 9.2 %fusion.2 = f32[9,9,2,1440]{3,0,2,1:T(8,128)S(1)} fusion(f32[9,9,2,1440]{3,1,2,0:T(8,128)S(1)} %fusion.21, f32[1440,1440,1,1]{1,0,3,2:T(8,128)S(1)} %bitcast.83), kind=kOutput, calls=%fused_computation.3 | convolution fusion | flops 4031078400 | bytes 10160640 | tf_op jit(solution)/shard_map/pfkc,ic->pfki/dot_general | solution.py:151
  178.3 2.4 %reshape.162 = f32[8,2,9,2,1440]{4,1,0,3,2:T(2,128)} reshape(f32[16,9,2,1440]{3,0,2,1:T(8,128)S(1)} %fusion.92) | data formatting | bytes 3317760 | tf_op jit(solution)/shard_map/reshape | solution.py:152
  180.6 3.5 %copy.45 = f32[8,2,9,2,1440]{4,1,3,2,0:T(2,128)} copy(f32[8,2,9,2,1440]{4,1,0,3,2:T(2,128)} %reshape.162) | data formatting | bytes 3317760 | tf_op jit(solution)/shard_map/reshape | solution.py:152
  184.1 5.6 %all-to-all-start.1 = ((f32[8,2,9,2,1440]{4,1,3,2,0:T(2,128)}), f32[8,2,9,2,1440]{4,1,3,2,0:T(2,128)S(1)}, u32[]{:S(2)}, u32[]{:S(2)}) async-start(f32[8,2,9,2,1440]{4,1,3,2,0:T(2,128)} %copy.45), calls=%async_computation.1 | async-start | bytes 3538944 | tf_op jit(solution)/shard_map/all_to_all | solution.py:155
  191.7 28.2 %all-to-all-done.1 = f32[8,2,9,2,1440]{4,1,3,2,0:T(2,128)S(1)} async-done(((f32[8,2,9,2,1440]{4,1,3,2,0:T(2,128)}), f32[8,2,9,2,1440]{4,1,3,2,0:T(2,128)S(1)}, u32[]{:S(2)}, u32[]{:S(2)}) %all-to-all-start.1) | async-done | bytes 1658912 | tf_op jit(solution)/shard_map/all_to_all | solution.py:155
  219.9 2.1 copy.46
  222.0 3.5 %reshape.163 = f32[16,9,2,1440]{3,0,2,1:T(8,128)} reshape(f32[8,2,9,2,1440]{4,1,0,3,2:T(2,128)} %copy.46) | data formatting | bytes 3317760 | tf_op jit(solution)/shard_map/reshape | solution.py:155
  225.5 2.8 %fusion.25 = f32[9,2,16,1440]{3,2,1,0:T(8,128)S(1)} fusion(f32[9,2,16,1440]{3,2,1,0:T(8,128)S(1)} %copy-done.2, f32[16,9,2,1440]{3,0,2,1:T(8,128)} %reshape.163, f32[8,2,16,1440]{3,2,1,0:T(8,128)S(1)} %broadcast_multiply_fusion, f32[1,2,16,1440]{3,2,1,0:T(8,128)S(1)} %bitcast.81, pred[16]{0:T(512)(128)(4,1)S(1)} %dynamic-slice_compare_fusion, ...), kind=kOutput, calls=%fused_computation.31 | convolution fusion | flops 80870656 | bytes 6635600 | tf_op jit(solution)/shard_map/ql,qfki->fkli/dot_general | solution.py:158
  (99 shorter events, 26.3 us)
Async XLA Ops:
  3.2 17.7 %collective-permute-start = (f32[11,2,1,1440]{3,2,1,0:T(1,128)}, f32[11,2,1,1440]{3,2,1,0:T(1,128)}, u32[]{:S(2)}, u32[]{:S(2)}) collective-permute-start(f32[11,2,1,1440]{3,2,1,0:T(1,128)} %get-tuple-element.14), channel_id=1, source_target_pairs={{4,0},{8,4},{12,8},{16,12},{20,16},{24,20},{28,24},{5,1},{9,5},{13... | collective-permute-start | bytes 380168 | tf_op jit(solution)/shard_map/ppermute | solution.py:25
  4.5 16.5 %collective-permute-start.1 = (f32[11,2,1,1440]{3,2,1,0:T(1,128)}, f32[11,2,1,1440]{3,2,1,0:T(1,128)}, u32[]{:S(2)}, u32[]{:S(2)}) collective-permute-start(f32[11,2,1,1440]{3,2,1,0:T(1,128)} %get-tuple-element.13), channel_id=1, source_target_pairs={{0,4},{4,8},{8,12},{12,16},{16,20},{20,24},{24,28},{1,5},{5,9},{9,... | collective-permute-start | bytes 380168 | tf_op jit(solution)/shard_map/ppermute | solution.py:23
  20.1 33.0 %copy-start.17 = (s32[16]{0:T(128)}, s32[16]{0:T(128)S(1)}, u32[]{:S(2)}) copy-start(s32[16]{0:T(128)S(1)} %dynamic_slice.7) | copy-start | bytes 196
  22.9 5.9 %copy-start.23 = (pred[128]{0:T(512)(128)(4,1)S(1)}, pred[128]{0:T(512)(128)(4,1)}, u32[]{:S(2)}) copy-start(pred[128]{0:T(512)(128)(4,1)} %get-tuple-element.3) | copy-start | bytes 388
  22.9 5.9 %copy-start.24 = (s32[128]{0:T(128)S(1)}, s32[128]{0:T(128)}, u32[]{:S(2)}) copy-start(s32[128]{0:T(128)} %get-tuple-element.22) | copy-start | bytes 1540
  22.9 5.9 %copy-start.25 = (s32[128]{0:T(128)S(1)}, s32[128]{0:T(128)}, u32[]{:S(2)}) copy-start(s32[128]{0:T(128)} %get-tuple-element.23) | copy-start | bytes 1540
  23.0 6.7 %copy-start.4 = (f32[2,16,1440]{2,1,0:T(8,128)S(1)}, f32[2,16,1440]{2,1,0:T(8,128)}, u32[]{:S(2)}) copy-start(f32[2,16,1440]{2,1,0:T(8,128)} %param.11) | copy-start | bytes 552964
  23.0 6.7 %copy-start.6 = (f32[2,16,1440]{2,1,0:T(8,128)S(1)}, f32[2,16,1440]{2,1,0:T(8,128)}, u32[]{:S(2)}) copy-start(f32[2,16,1440]{2,1,0:T(8,128)} %param.10) | copy-start | bytes 552964
  24.2 18.0 %collective-permute-start.3 = (f32[11,1,18,1440]{3,1,2,0:T(1,128)S(1)}, f32[11,1,18,1440]{3,1,2,0:T(1,128)S(1)}, u32[]{:S(2)}, u32[]{:S(2)}) collective-permute-start(f32[11,1,18,1440]{3,1,2,0:T(1,128)S(1)} %copy.36), channel_id=1, source_target_pairs={{0,1},{1,2},{2,3},{4,5},{5,6},{6,7},{8,9},{9,10},{10,11},{12,13},{... | collective-permute-start | bytes 3421448 | tf_op jit(solution)/shard_map/ppermute | solution.py:23
  31.0 17.9 %collective-permute-start.2 = (f32[11,1,18,1440]{3,1,2,0:T(1,128)S(1)}, f32[11,1,18,1440]{3,1,2,0:T(1,128)S(1)}, u32[]{:S(2)}, u32[]{:S(2)}) collective-permute-start(f32[11,1,18,1440]{3,1,2,0:T(1,128)S(1)} %copy.34), channel_id=1, source_target_pairs={{1,0},{2,1},{3,2},{5,4},{6,5},{7,6},{9,8},{10,9},{11,10},{13,12},{... | collective-permute-start | bytes 3421448 | tf_op jit(solution)/shard_map/ppermute | solution.py:25
  43.2 5.8 %copy-start.7 = (f32[9,2,16,1]{3,2,1,0:T(8,128)S(1)}, f32[9,2,16,1]{3,2,1,0:T(8,128)}, u32[]{:S(2)}) copy-start(f32[9,2,16,1]{3,2,1,0:T(8,128)} %slice.82) | copy-start | bytes 3460
  43.2 5.8 %copy-start.19 = (f32[16]{0:T(128)S(1)}, f32[16]{0:T(128)}, u32[]{:S(2)}) copy-start(f32[16]{0:T(128)} %get-tuple-element.28) | copy-start | bytes 196
  43.2 5.8 %copy-start.20 = (f32[16]{0:T(128)S(1)}, f32[16]{0:T(128)}, u32[]{:S(2)}) copy-start(f32[16]{0:T(128)} %get-tuple-element.29) | copy-start | bytes 196
  43.3 5.8 %copy-start.21 = (f32[2]{0:T(128)S(1)}, f32[2]{0:T(128)}, u32[]{:S(2)}) copy-start(f32[2]{0:T(128)} %get-tuple-element.24) | copy-start | bytes 28
  43.3 5.8 %copy-start.22 = (f32[2]{0:T(128)S(1)}, f32[2]{0:T(128)}, u32[]{:S(2)}) copy-start(f32[2]{0:T(128)} %get-tuple-element.25) | copy-start | bytes 28
  60.9 82.5 %all-to-all-start = ((f32[8,2,9,2,1440]{4,1,3,2,0:T(2,128)}), f32[8,2,9,2,1440]{4,1,3,2,0:T(2,128)S(1)}, u32[]{:S(2)}, u32[]{:S(2)}) async-start(f32[8,2,9,2,1440]{4,1,3,2,0:T(2,128)} %copy.39), calls=%async_computation | async-start | bytes 3538944 | tf_op jit(solution)/shard_map/all_to_all | solution.py:142
  66.0 39.1 %copy-start.12 = (pred[1440]{0:T(1024)(128)(4,1)S(1)}, pred[1440]{0:T(1024)(128)(4,1)}, u32[]{:S(2)}) copy-start(pred[1440]{0:T(1024)(128)(4,1)} %iota_compare_fusion.5) | copy-start | bytes 4324
  144.3 23.0 %slice-start = ((s8[8847360]{0:T(1024)(128)(4,1)}), s8[4194304]{0:T(1024)(128)(4,1)S(1)}, s32[]{:S(2)}) async-start(s8[8847360]{0:T(1024)(128)(4,1)} %bitcast.82), calls=%async_computation.2 | async-start | bytes 8388608
  146.0 21.3 %slice-start.1 = ((s8[8847360]{0:T(1024)(128)(4,1)}), s8[4194304]{0:T(1024)(128)(4,1)S(1)}, s32[]{:S(2)}) async-start(s8[8847360]{0:T(1024)(128)(4,1)} %bitcast.82), calls=%async_computation.3 | async-start | bytes 8388608
  146.0 21.3 %slice-start.2 = ((s8[8847360]{0:T(1024)(128)(4,1)}), s8[458752]{0:T(1024)(128)(4,1)S(1)}, s32[]{:S(2)}) async-start(s8[8847360]{0:T(1024)(128)(4,1)} %bitcast.82), calls=%async_computation.4 | async-start | bytes 917504
  167.4 9.2 %copy-start.13 = (f32[9,9,2,1440]{3,1,2,0:T(8,128)}, f32[9,9,2,1440]{3,1,2,0:T(8,128)S(1)}, u32[]{:S(2)}) copy-start(f32[9,9,2,1440]{3,1,2,0:T(8,128)S(1)} %fusion.21) | copy-start | bytes 2799364
  184.1 5.6 %copy-start.16 = (s32[128]{0:T(128)S(1)}, s32[128]{0:T(128)}, u32[]{:S(2)}) copy-start(s32[128]{0:T(128)} %param.12) | copy-start | bytes 1540
  184.1 35.8 %all-to-all-start.1 = ((f32[8,2,9,2,1440]{4,1,3,2,0:T(2,128)}), f32[8,2,9,2,1440]{4,1,3,2,0:T(2,128)S(1)}, u32[]{:S(2)}, u32[]{:S(2)}) async-start(f32[8,2,9,2,1440]{4,1,3,2,0:T(2,128)} %copy.45), calls=%async_computation.1 | async-start | bytes 3538944 | tf_op jit(solution)/shard_map/all_to_all | solution.py:155
  222.0 3.5 %copy-start.18 = (s32[16]{0:T(128)S(1)}, s32[16]{0:T(128)}, u32[]{:S(2)}) copy-start(s32[16]{0:T(128)} %copy-done.17) | copy-start | bytes 196
  (11 other events, 25.0 us)
where the time goes:
time: 234 us; the launch traced here: 230 us
  other arithmetic  96.3 us (41%)
  waiting for transfers between devices  42.4 us (18%)
  matrix products  40.5 us (17%)
  local copies, waits for them, and re-layouts  26.3 us (11%)
  starting transfers between devices  23.6 us (10%)
    dot_general x1, other arithmetic, local(): jnp.einsum('pfki,ic->pfkc', slot_data, dft_table, precision=highest)  39.1 us
    dot_general x1, other arithmetic, local(): restored = jnp.einsum('pfkc,ic->pfki', coeffs, dft_table, precision=highest)  38.3 us
    all_to_all x1, waiting for transfers between devices, local(): lax.all_to_all(returning, 'lat', split_axis=0, concat_axis=0, tiled=True)  28.2 us
    dot_general x1, matrix products, local(): jnp.einsum('pfki,ic->pfkc', slot_data, dft_table, precision=highest)  21.3 us
    ppermute x2, starting transfers between devices, padded_2(): lax.ppermute(tail, axis, [(i, (i + 1) % count) for i in range(ends)])  9.74 us
    dot_general x1, matrix products, local(): restored = jnp.einsum('pfkc,ic->pfki', coeffs, dft_table, precision=highest)  9.22 us
    ppermute x2, waiting for transfers between devices, padded_2(): lax.ppermute(tail, axis, [(i, (i + 1) % count) for i in range(ends)])  8.64 us
    reshape x2, local copies, waits for them, and re-layouts, local(): jnp.einsum('pq,pfki->qfki', collect_map, restored, precision=highest)  5.85 us
  transfers between devices with their start and end apart: 6, of which 3 were waited for; matrix products, arithmetic and copies ran while one was open for 41% of the time, Pallas kernels for 0%

commit v1 on v0

v1 whole, which is shorter than its diff:
```python
import math

import jax
import jax.numpy as jnp
import numpy as np
from jax import lax
from jax.sharding import PartitionSpec as P

PI = math.pi
COS_CUT = math.cos(40.0 * math.pi / 180.0)


def spectral_table(nlon):
    ids = np.arange(nlon)
    nyquist = nlon // 2
    wave = np.where(ids <= nyquist, ids, ids - nyquist)
    angles = (ids[:, None] * wave[None, :] % nlon) * (2.0 * PI / nlon)
    weights = np.where((ids == 0) | (ids == nyquist), math.sqrt(1.0 / nlon), math.sqrt(2.0 / nlon))
    return np.where(ids[None, :] <= nyquist, np.cos(angles), np.sin(angles)) * weights[None, :]


def sine_wave(nlon):
    ids = np.arange(nlon)
    nyquist = nlon // 2
    wave = np.where(ids <= nyquist, ids, ids - nyquist)
    return np.abs(np.sin(wave * (PI / nlon))).astype(np.float32)


def cell_cosine(row_ids, total_rows):
    return jnp.cos((row_ids.astype(jnp.float32) + 0.5) * (PI / total_rows) - 0.5 * PI)


def face_cosine(row_ids, total_rows):
    return jnp.sin((row_ids + 1).astype(jnp.float32) * (PI / total_rows)) * (
        row_ids + 1 < total_rows
    ).astype(jnp.float32)


def upwind(courant, first, second):
    return jnp.maximum(courant, 0.0) * first + jnp.minimum(courant, 0.0) * second


def split(x):
    hi = lax.reduce_precision(x, 8, 7)
    lo = lax.reduce_precision(x - hi, 8, 7)
    return hi.astype(jnp.bfloat16), lo.astype(jnp.bfloat16)


def product(x, hi, lo, contract):
    dims = (((x.ndim - 1,), (contract,)), ((), ()))
    xh, xl = split(x)
    dot = lambda a, b: lax.dot_general(a, b, dims, preferred_element_type=jnp.float32)
    return dot(xh, hi) + (dot(xl, hi) + dot(xh, lo))


def shifted(x, axis, up):
    count = lax.axis_size(axis)
    pairs = [(i, i + 1) if up else (i + 1, i) for i in range(count - 1)]
    return lax.ppermute(x, axis, pairs)


def spectra_maps(filter_flags, owner_slots, my_band, lat_dev, lat_count, slot_dev):
    total_rows = filter_flags.shape[0]
    cap = -(-lat_dev // lat_count)
    flagged = filter_flags == 1
    owner = jnp.where(flagged, owner_slots // slot_dev, -1)
    place = jnp.where(flagged, owner_slots % slot_dev, 0)
    rows = jnp.arange(total_rows, dtype=jnp.int32)
    source = rows // lat_dev
    earlier = (
        (source[:, None] == source[None, :])
        & (owner[:, None] == owner[None, :])
        & (rows[None, :] < rows[:, None])
    )
    rank = jnp.sum(earlier.astype(jnp.int32), axis=1)
    buffer = jnp.arange(lat_count * cap, dtype=jnp.int32)
    sends = (
        (source[None, :] == my_band)
        & flagged[None, :]
        & ((owner * cap + rank)[None, :] == buffer[:, None])
    )
    pick = jnp.sum(jnp.where(sends, (rows % lat_dev)[None, :], 0), axis=1)
    slots = jnp.arange(slot_dev, dtype=jnp.int32)
    takes = flagged[None, :] & (owner[None, :] == my_band) & (place[None, :] == slots[:, None])
    collect = jnp.sum(jnp.where(takes, (source * cap + rank)[None, :], 0), axis=1)
    return pick, collect


def local(thickness, tracers, east_courant, north_courant, vert_courant, filter_flags, owner_slots, hi, lo):
    lev_dev, lat_dev, nlon = thickness.shape
    lat_count = lax.axis_size("lat")
    lev_count = lax.axis_size("lev")
    slot_dev = 9
    my_band = lax.axis_index("lat")
    my_levels = lax.axis_index("lev")
    total_rows = lat_dev * lat_count
    total_levels = lev_dev * lev_count
    fields = jnp.concatenate([thickness[None], thickness[None] * tracers], axis=0)
    row_last = jnp.concatenate([fields[:, :, -1:], north_courant[None, :, -1:]], axis=0)
    lev_last = jnp.concatenate([fields[:, -1:], vert_courant[None, -1:]], axis=0)
    from_south = shifted(row_last, "lat", True)
    from_north = shifted(fields[:, :, :1], "lat", False)
    from_above = shifted(lev_last, "lev", True)
    from_below = shifted(fields[:, :1], "lev", False)
    rows = my_band * lat_dev + jnp.arange(lat_dev, dtype=jnp.int32)
    levels = my_levels * lev_dev + jnp.arange(lev_dev, dtype=jnp.int32)
    east_flux = upwind(east_courant, fields, jnp.roll(fields, -1, axis=3))
    div_east = east_flux - jnp.roll(east_flux, 1, axis=3)
    x_north = jnp.concatenate([fields[:, :, 1:], from_north], axis=2)
    x_south = jnp.concatenate([from_south[:-1], fields[:, :, :-1]], axis=2)
    south_courant = jnp.concatenate([from_south[-1], north_courant[:, :-1]], axis=1)
    north_flux = upwind(north_courant, fields, x_north) * face_cosine(rows, total_rows)[:, None]
    north_prev = upwind(south_courant, x_south, fields) * face_cosine(rows - 1, total_rows)[:, None]
    div_north = (north_flux - north_prev) / cell_cosine(rows, total_rows)[:, None]
    x_below = jnp.concatenate([fields[:, 1:], from_below], axis=1)
    x_above = jnp.concatenate([from_above[:-1], fields[:, :-1]], axis=1)
    above_courant = jnp.concatenate([from_above[-1], vert_courant[:-1]], axis=0)
    mask = (levels + 1 < total_levels).astype(jnp.float32)[:, None, None]
    div_vert = upwind(vert_courant, fields, x_below) * mask - upwind(above_courant, x_above, fields)
    change = -(div_east + div_north + div_vert)
    ratio = (cell_cosine(rows, total_rows) / COS_CUT)[:, None]
    fraction = ratio / jnp.maximum(ratio, jnp.asarray(sine_wave(nlon))[None, :])
    coeffs = product(change, hi, lo, 0) * (fraction * fraction)
    restored = product(coeffs, hi, lo, 1)
    flags = lax.dynamic_slice_in_dim(filter_flags, my_band * lat_dev, lat_dev) == 1
    updated = fields + jnp.where(flags[None, None, :, None], restored, change)
    pick, collect = spectra_maps(filter_flags, owner_slots, my_band, lat_dev, lat_count, slot_dev)
    outgoing = jnp.take(coeffs[0], pick, axis=1).transpose(1, 0, 2)
    arrived = lax.all_to_all(outgoing, "lat", split_axis=0, concat_axis=0, tiled=True)
    spectra = jnp.take(arrived, collect, axis=0)
    return (updated[0], updated[1:], spectra)


def solution(mesh):
    def run(thickness, tracers, east_courant, north_courant, vert_courant, filter_flags, owner_slots):
        table = spectral_table(thickness.shape[-1]).astype(np.float32)
        high = table.astype(jnp.bfloat16)
        low = (table - high.astype(np.float32)).astype(jnp.bfloat16)
        mapped = jax.shard_map(
            local,
            mesh=mesh,
            in_specs=(
                P("lev", "lat", None),
                P(None, "lev", "lat", None),
                P("lev", "lat", None),
                P("lev", "lat", None),
                P("lev", "lat", None),
                P(),
                P(),
                P(),
                P(),
            ),
            out_specs=(P("lev", "lat", None), P(None, "lev", "lat", None), P("lat", "lev", None)),
            check_vma=False,
        )
        return mapped(
            thickness,
            tracers,
            east_courant,
            north_courant,
            vert_courant,
            filter_flags,
            owner_slots,
            jnp.asarray(high),
            jnp.asarray(low),
        )

    return run
```

time: 234 us -> 72 us (0.31)
  the two profiles are of different devices: /device:TPU:1 before, /device:TPU:0 now
where the time goes in v1:
time: 72 us; the launch traced here: 71.5 us
  other arithmetic  25.1 us (35%)
  starting transfers between devices  17.7 us (25%)
  matrix products  9.77 us (14%)
  local copies, waits for them, and re-layouts  9.43 us (13%)
  waiting for transfers between devices  8.33 us (12%)
  between operations  1.1 us (2%)
    ppermute x4, starting transfers between devices, shifted(): return lax.ppermute(x, axis, pairs)  10.8 us
    dot_general x6, matrix products, product(): lax.dot_general(a, b, dims, preferred_element_type=jnp.float32)  9.77 us
    all_to_all x1, waiting for transfers between devices, local(): lax.all_to_all(outgoing, 'lat', split_axis=0, concat_axis=0, tiled=True)  8.32 us
    all_to_all x1, starting transfers between devices, local(): lax.all_to_all(outgoing, 'lat', split_axis=0, concat_axis=0, tiled=True)  6.95 us
    concatenate x5, other arithmetic, local(): jnp.concatenate([thickness[None], thickness[None] * tracers], axis=0)  6.44 us
    neg x1, other arithmetic, local(): change = -(div_east + div_north + div_vert)  3.94 us
    max x4, other arithmetic, upwind(): jnp.maximum(courant, 0.0) * first + jnp.minimum(courant, 0.0) * second  3.54 us
    add x1, other arithmetic, upwind(): jnp.maximum(courant, 0.0) * first + jnp.minimum(courant, 0.0) * second  1.97 us
  transfers between devices with their start and end apart: 5, of which 1 were waited for; matrix products, arithmetic and copies ran while one was open for 29% of the time, Pallas kernels for 0%

profile of v1, /device:TPU:0, one launch (start us, length us, event | category | flops | bytes accessed | tf_op | source)
XLA Modules:
  0.0 71.5 jit_solution(17839750952797922794)
XLA Ops:
  0.6 1.6 %fusion.49 = (f32[1,16,1440]{2,1,0:T(8,128)}, f32[1,1,16,1440]{3,2,1,0:T(8,128)S(1)}) fusion(f32[2,16,1440]{2,1,0:T(8,128)} %param.14), kind=kLoop, calls=%fused_computation.127 | loop fusion | bytes 368640 | tf_op jit(solution)/shard_map/slice | solution.py:117
  2.2 1.6 %broadcast_multiply_fusion = f32[8,2,16,1440]{3,2,1,0:T(8,128)S(1)} fusion(f32[8,2,16,1440]{3,2,1,0:T(8,128)} %param.11, f32[2,16,1440]{2,1,0:T(8,128)} %param.10), kind=kLoop, calls=%fused_computation.59 | loop fusion | flops 368640 | bytes 3133440 | tf_op jit(solution)/shard_map/mul | solution.py:98
  3.8 1.1 %fusion.26 = (f32[9,1,16,1440]{3,2,1,0:T(8,128)S(1)}, f32[9,1,16,1440]{3,2,1,0:T(8,128)}) fusion(f32[8,2,16,1440]{3,2,1,0:T(8,128)S(1)} %broadcast_multiply_fusion, f32[1,2,16,1440]{3,2,1,0:T(8,128)S(1)} %bitcast.36), kind=kLoop, calls=%fused_computation.55 | loop fusion | flops 414720 | bytes 3317760 | tf_op jit(solution)/shard_map/concatenate | solution.py:98
  4.9 1.0 %pad_maximum_fusion.1 = f32[10,1,16,1440]{3,2,1,0:T(8,128)} fusion(f32[1,1,16,1440]{3,2,1,0:T(8,128)S(1)} %get-tuple-element.23, f32[9,1,16,1440]{3,2,1,0:T(8,128)S(1)} %get-tuple-element.8), kind=kLoop, calls=%fused_computation.54 | loop fusion | flops 230400 | bytes 1843200 | tf_op jit(solution)/shard_map/concatenate | solution.py:100
  5.9 3.3 %collective-permute-start.3 = (f32[10,1,16,1440]{3,2,1,0:T(8,128)}, f32[10,1,16,1440]{3,2,1,0:T(8,128)}, u32[]{:S(2)}, u32[]{:S(2)}) collective-permute-start(f32[10,1,16,1440]{3,2,1,0:T(8,128)} %pad_maximum_fusion.1), channel_id=1, source_target_pairs={{0,1},{1,2},{2,3},{4,5},{5,6},{6,7},{8,9},{9,10},{10,11},{12,13},{... | collective-permute-start | bytes 2764808 | tf_op jit(solution)/shard_map/ppermute | solution.py:59
  10.8 4.9 %collective-permute-start.1 = (f32[10,2,1,1440]{3,2,1,0:T(1,128)}, f32[10,2,1,1440]{3,2,1,0:T(1,128)}, u32[]{:S(2)}, u32[]{:S(2)}) collective-permute-start(f32[10,2,1,1440]{3,2,1,0:T(1,128)} %pad_maximum_fusion.4), channel_id=1, source_target_pairs={{0,4},{4,8},{8,12},{12,16},{16,20},{20,24},{24,28},{1,5},{5,9},{9,... | collective-permute-start | bytes 345608 | tf_op jit(solution)/shard_map/ppermute | solution.py:59
  15.7 1.3 %collective-permute-start.2 = (f32[9,1,16,1440]{3,2,1,0:T(8,128)}, f32[9,1,16,1440]{3,2,1,0:T(8,128)}, u32[]{:S(2)}, u32[]{:S(2)}) collective-permute-start(f32[9,1,16,1440]{3,2,1,0:T(8,128)} %get-tuple-element.9), channel_id=1, source_target_pairs={{1,0},{2,1},{3,2},{5,4},{6,5},{7,6},{9,8},{10,9},{11,10},{13,12},{... | collective-permute-start | bytes 2488328 | tf_op jit(solution)/shard_map/ppermute | solution.py:59
  17.0 1.3 %collective-permute-start = (f32[9,2,1,1440]{3,2,1,0:T(1,128)}, f32[9,2,1,1440]{3,2,1,0:T(1,128)}, u32[]{:S(2)}, u32[]{:S(2)}) collective-permute-start(f32[9,2,1,1440]{3,2,1,0:T(1,128)} %get-tuple-element.11), channel_id=1, source_target_pairs={{4,0},{8,4},{12,8},{16,12},{20,16},{24,20},{28,24},{5,1},{9,5},{13... | collective-permute-start | bytes 311048 | tf_op jit(solution)/shard_map/ppermute | solution.py:59
  18.3 1.8 %fusion.9 = f32[9,2,16,1439]{3,2,1,0:T(8,128)} fusion(f32[1,2,16,1440]{3,2,1,0:T(8,128)S(1)} %bitcast.38, f32[8,2,16,1440]{3,2,1,0:T(8,128)S(1)} %broadcast_multiply_fusion), kind=kLoop, calls=%fused_computation.26 | loop fusion | flops 414432 | bytes 3316608 | tf_op jit(solution)/shard_map/concatenate | solution.py:98
  20.8 2.1 %fusion.11 = (f32[9,2,15,1440]{3,2,1,0:T(8,128)}, f32[9,2,15,1440]{3,2,1,0:T(8,128)}) fusion(f32[1,2,16,1440]{3,2,1,0:T(8,128)S(1)} %bitcast.40, f32[8,2,16,1440]{3,2,1,0:T(8,128)S(1)} %broadcast_multiply_fusion), kind=kLoop, calls=%fused_computation.28 | loop fusion | flops 777600 | bytes 4769280 | tf_op jit(solution)/shard_map/concatenate | solution.py:98
  27.5 2.0 %fusion.12 = f32[9,2,16,1440]{3,2,1,0:T(8,128)S(1)} fusion(f32[9,2,16,1]{3,2,1,0:T(8,128)} %fusion.38, f32[9,2,16,1439]{3,2,1,0:T(8,128)} %fusion.9, f32[8,2,16,1440]{3,2,1,0:T(8,128)S(1)} %broadcast_multiply_fusion, f32[1,2,16,1440]{3,2,1,0:T(8,128)S(1)} %bitcast.41, f32[2,16,1440]{2,1,0:T(8,128)} %get-tuple-element.25, f32[2,16,1440]{2,1,0:T(8,128)} %get-tuple-element.24), kind=kLoop, calls=%fused_computation.30 | loop fusion | flops 2073600 | bytes 5345280 | tf_op jit(solution)/shard_map/add | solution.py:40
  31.0 1.1 %slice.107 = f32[9,2,1,1440]{3,2,1,0:T(1,128)S(1)} slice(f32[10,2,1,1440]{3,2,1,0:T(1,128)} %collective-permute-done.1), slice={[0:9], [0:2], [0:1], [0:1440]} | slice | bytes 207360 | tf_op jit(solution)/shard_map/slice | solution.py:110
  32.8 1.0 %fusion.37 = (f32[2,16,1440]{2,1,0:T(8,128)S(1)}, f32[2,16,1440]{2,1,0:T(8,128)S(1)}) fusion(f32[2,15,1440]{2,1,0:T(8,128)} %bitcast.46, f32[2,1,1440]{2,1,0:T(1,128)S(1)} %slice_bitcast_fusion.4), kind=kLoop, calls=%fused_computation.70 | loop fusion | flops 138240 | bytes 552960 | tf_op jit(solution)/shard_map/max | solution.py:40
  35.6 1.4 %slice.115 = f32[9,1,16,1440]{3,2,1,0:T(8,128)S(1)} slice(f32[10,1,16,1440]{3,2,1,0:T(8,128)} %collective-permute-done.3), slice={[0:9], [0:1], [0:16], [0:1440]} | slice | bytes 1658880 | tf_op jit(solution)/shard_map/slice | solution.py:116
  37.2 3.9 %fusion.15 = f32[9,2,16,1440]{3,2,1,0:T(8,128)S(1)} fusion(f32[9,2,16,1440]{3,2,1,0:T(8,128)S(1)} %fusion.12, f32[9,2,16,1439]{3,2,1,0:T(8,128)S(1)} %bitcast.35, f32[9,2,16,1]{3,2,1,0:T(8,128)S(1)} %slice.98, f32[9,2,1,1440]{3,2,1,0:T(1,128)} %collective-permute-done, f32[9,2,15,1440]{3,2,1,0:T(8,128)} %get-tuple-element.13, ...), kind=kLoop, calls=%fused_computation.34 | loop fusion | flops 11612160 | bytes 14745800 | tf_op jit(solution)/shard_map/neg | solution.py:120
  41.2 1.5 %fusion.30 = f32[9,2,16,1440]{3,2,1,0:T(8,128)S(1)} fusion(bf16[1440,1440,1,1]{1,0,3,2:T(8,128)(2,1)S(1)} %bitcast.48, f32[9,2,16,1440]{3,2,1,0:T(8,128)S(1)} %fusion.15), kind=kOutput, calls=%fused_computation.58 | convolution fusion | flops 1196052480 | bytes 7464960 | tf_op jit(solution)/shard_map/dot_general | solution.py:52
  42.7 1.5 %fusion.32 = f32[9,2,16,1440]{3,2,1,0:T(8,128)S(1)} fusion(bf16[1440,1440,1,1]{1,0,3,2:T(8,128)(2,1)S(1)} %bitcast.48, f32[9,2,16,1440]{3,2,1,0:T(8,128)S(1)} %fusion.15), kind=kOutput, calls=%fused_computation.60 | convolution fusion | flops 1195223040 | bytes 7464960 | tf_op jit(solution)/shard_map/dot_general | solution.py:52
  44.3 1.6 %fusion.4 = f32[9,2,16,1440]{3,2,1,0:T(8,128)S(1)} fusion(f32[9,2,16,1440]{3,2,1,0:T(8,128)S(1)} %fusion.32, f32[9,2,16,1440]{3,2,1,0:T(8,128)S(1)} %fusion.30, bf16[1440,1440,1,1]{1,0,3,2:T(8,128)(2,1)S(1)} %bitcast.45, f32[16,1440]{1,0:T(8,128)S(1)} %copy-done.10, f32[9,2,16,1440]{3,2,1,0:T(8,128)S(1)} %fusion.15), kind=kOutput, calls=%fused_computation.17 | convolution fusion | flops 1196467200 | bytes 10874880 | tf_op jit(solution)/shard_map/dot_general | solution.py:52
  45.9 1.6 %fusion.28 = f32[9,2,16,1440]{3,2,1,0:T(8,128)S(1)} fusion(bf16[1440,1440,1,1]{1,0,3,2:T(8,128)(2,1)S(1)} %bitcast.48, f32[9,2,16,1440]{3,2,1,0:T(8,128)S(1)} %fusion.4), kind=kOutput, calls=%fused_computation.57 | convolution fusion | flops 1196052480 | bytes 7464960 | tf_op jit(solution)/shard_map/dot_general | solution.py:52
  47.5 1.6 %fusion.33 = f32[9,2,16,1440]{3,2,1,0:T(8,128)S(1)} fusion(bf16[1440,1440,1,1]{1,0,3,2:T(8,128)(2,1)S(1)} %bitcast.48, f32[9,2,16,1440]{3,2,1,0:T(8,128)S(1)} %fusion.4), kind=kOutput, calls=%fused_computation.61 | convolution fusion | flops 1195223040 | bytes 7464960 | tf_op jit(solution)/shard_map/dot_general | solution.py:52
  49.1 1.9 %fusion.2 = f32[9,2,16,1440]{3,2,1,0:T(8,128)S(1)} fusion(f32[9,2,16,1440]{3,2,1,0:T(8,128)S(1)} %fusion.15, f32[9,2,16,1440]{3,2,1,0:T(8,128)S(1)} %fusion.33, f32[9,2,16,1440]{3,2,1,0:T(8,128)S(1)} %fusion.28, bf16[1440,1440,1,1]{1,0,3,2:T(8,128)(2,1)S(1)} %bitcast.45, f32[8,2,16,1440]{3,2,1,0:T(8,128)S(1)} %broadcast_multiply_fusion, ...), kind=kOutput, calls=%fused_computation.14 | convolution fusion | flops 1197296640 | bytes 14100496 | tf_op jit(solution)/shard_map/dot_general | solution.py:52
  51.0 1.3 %slice.117 = f32[8,2,16,1440]{3,2,1,0:T(8,128)} slice(f32[9,2,16,1440]{3,2,1,0:T(8,128)S(1)} %fusion.2), slice={[1:9], [0:2], [0:16], [0:1440]} | slice | bytes 2949120 | tf_op jit(solution)/shard_map/slice | solution.py:131
  54.1 7.0 %all-to-all-start = ((f32[16,2,1440]{2,1,0:T(2,128)}), f32[16,2,1440]{2,1,0:T(2,128)S(1)}, u32[]{:S(2)}, u32[]{:S(2)}) async-start(f32[16,2,1440]{2,1,0:T(2,128)} %broadcast_select_fusion), calls=%async_computation | async-start | bytes 393216 | tf_op jit(solution)/shard_map/all_to_all | solution.py:129
  61.7 8.3 %all-to-all-done = f32[16,2,1440]{2,1,0:T(2,128)S(1)} async-done(((f32[16,2,1440]{2,1,0:T(2,128)}), f32[16,2,1440]{2,1,0:T(2,128)S(1)}, u32[]{:S(2)}, u32[]{:S(2)}) %all-to-all-start) | async-done | bytes 184352 | tf_op jit(solution)/shard_map/all_to_all | solution.py:129
  (89 shorter events, 14.8 us)
Async XLA Ops:
  4.9 5.2 %copy-start.1 = (f32[9,1,16,1440]{3,2,1,0:T(8,128)}, f32[9,1,16,1440]{3,2,1,0:T(8,128)S(1)}, u32[]{:S(2)}) copy-start(f32[9,1,16,1440]{3,2,1,0:T(8,128)S(1)} %get-tuple-element.8) | copy-start | bytes 2488324
  4.9 5.2 %copy-start.4 = (f32[2,16,1440]{2,1,0:T(8,128)S(1)}, f32[2,16,1440]{2,1,0:T(8,128)}, u32[]{:S(2)}) copy-start(f32[2,16,1440]{2,1,0:T(8,128)} %param.13) | copy-start | bytes 552964
  5.9 27.9 %collective-permute-start.3 = (f32[10,1,16,1440]{3,2,1,0:T(8,128)}, f32[10,1,16,1440]{3,2,1,0:T(8,128)}, u32[]{:S(2)}, u32[]{:S(2)}) collective-permute-start(f32[10,1,16,1440]{3,2,1,0:T(8,128)} %pad_maximum_fusion.1), channel_id=1, source_target_pairs={{0,1},{1,2},{2,3},{4,5},{5,6},{6,7},{8,9},{9,10},{10,11},{12,13},{... | collective-permute-start | bytes 2764808 | tf_op jit(solution)/shard_map/ppermute | solution.py:59
  10.8 20.2 %collective-permute-start.1 = (f32[10,2,1,1440]{3,2,1,0:T(1,128)}, f32[10,2,1,1440]{3,2,1,0:T(1,128)}, u32[]{:S(2)}, u32[]{:S(2)}) collective-permute-start(f32[10,2,1,1440]{3,2,1,0:T(1,128)} %pad_maximum_fusion.4), channel_id=1, source_target_pairs={{0,4},{4,8},{8,12},{12,16},{16,20},{20,24},{24,28},{1,5},{5,9},{9,... | collective-permute-start | bytes 345608 | tf_op jit(solution)/shard_map/ppermute | solution.py:59
  15.7 21.3 %collective-permute-start.2 = (f32[9,1,16,1440]{3,2,1,0:T(8,128)}, f32[9,1,16,1440]{3,2,1,0:T(8,128)}, u32[]{:S(2)}, u32[]{:S(2)}) collective-permute-start(f32[9,1,16,1440]{3,2,1,0:T(8,128)} %get-tuple-element.9), channel_id=1, source_target_pairs={{1,0},{2,1},{3,2},{5,4},{6,5},{7,6},{9,8},{10,9},{11,10},{13,12},{... | collective-permute-start | bytes 2488328 | tf_op jit(solution)/shard_map/ppermute | solution.py:59
  17.0 20.0 %collective-permute-start = (f32[9,2,1,1440]{3,2,1,0:T(1,128)}, f32[9,2,1,1440]{3,2,1,0:T(1,128)}, u32[]{:S(2)}, u32[]{:S(2)}) collective-permute-start(f32[9,2,1,1440]{3,2,1,0:T(1,128)} %get-tuple-element.11), channel_id=1, source_target_pairs={{4,0},{8,4},{12,8},{16,12},{20,16},{24,20},{28,24},{5,1},{9,5},{13... | collective-permute-start | bytes 311048 | tf_op jit(solution)/shard_map/ppermute | solution.py:59
  20.8 4.2 %copy-start.17 = (s32[128]{0:T(128)S(1)}, s32[128]{0:T(128)}, u32[]{:S(2)}) copy-start(s32[128]{0:T(128)} %param.16) | copy-start | bytes 1540
  20.8 4.2 %copy-start.18 = (s32[128]{0:T(128)S(1)}, s32[128]{0:T(128)}, u32[]{:S(2)}) copy-start(s32[128]{0:T(128)} %param.15) | copy-start | bytes 1540
  20.8 5.3 %copy-start.11 = (f32[2,16,1440]{2,1,0:T(8,128)S(1)}, f32[2,16,1440]{2,1,0:T(8,128)}, u32[]{:S(2)}) copy-start(f32[2,16,1440]{2,1,0:T(8,128)} %param.12) | copy-start | bytes 552964
  22.9 3.9 %copy-start.12 = (f32[1440]{0:T(1024)S(1)}, f32[1440]{0:T(1024)}, u32[]{:S(2)}) copy-start(f32[1440]{0:T(1024)} %constant.118.clone) | copy-start | bytes 17284
  30.1 6.9 %copy-start.8 = (f32[2,16,1440]{2,1,0:T(8,128)S(1)}, f32[2,16,1440]{2,1,0:T(8,128)}, u32[]{:S(2)}) copy-start(f32[2,16,1440]{2,1,0:T(8,128)} %get-tuple-element.34) | copy-start | bytes 552964
  30.2 6.9 %copy-start.2 = (f32[9,1,16,1440]{3,2,1,0:T(8,128)S(1)}, f32[9,1,16,1440]{3,2,1,0:T(8,128)}, u32[]{:S(2)}) copy-start(f32[9,1,16,1440]{3,2,1,0:T(8,128)} %copy-done.1) | copy-start | bytes 2488324
  30.2 6.9 %copy-start.3 = (f32[9,2,15,1440]{3,2,1,0:T(8,128)S(1)}, f32[9,2,15,1440]{3,2,1,0:T(8,128)}, u32[]{:S(2)}) copy-start(f32[9,2,15,1440]{3,2,1,0:T(8,128)} %get-tuple-element.12) | copy-start | bytes 4665604
  30.2 6.9 %copy-start.5 = (f32[2,16,1440]{2,1,0:T(8,128)S(1)}, f32[2,16,1440]{2,1,0:T(8,128)}, u32[]{:S(2)}) copy-start(f32[2,16,1440]{2,1,0:T(8,128)} %get-tuple-element.18) | copy-start | bytes 552964
  30.2 6.9 %copy-start.6 = (f32[2,16,1440]{2,1,0:T(8,128)S(1)}, f32[2,16,1440]{2,1,0:T(8,128)}, u32[]{:S(2)}) copy-start(f32[2,16,1440]{2,1,0:T(8,128)} %get-tuple-element.19) | copy-start | bytes 552964
  30.2 6.9 %copy-start.7 = (f32[2,16,1440]{2,1,0:T(8,128)S(1)}, f32[2,16,1440]{2,1,0:T(8,128)}, u32[]{:S(2)}) copy-start(f32[2,16,1440]{2,1,0:T(8,128)} %get-tuple-element.33) | copy-start | bytes 552964
  30.3 6.9 %copy-start.13 = (f32[16]{0:T(128)S(1)}, f32[16]{0:T(128)}, u32[]{:S(2)}) copy-start(f32[16]{0:T(128)} %get-tuple-element.29) | copy-start | bytes 196
  30.3 6.9 %copy-start.14 = (f32[16]{0:T(128)S(1)}, f32[16]{0:T(128)}, u32[]{:S(2)}) copy-start(f32[16]{0:T(128)} %get-tuple-element.30) | copy-start | bytes 196
  30.3 6.9 %copy-start.15 = (f32[16]{0:T(128)S(1)}, f32[16]{0:T(128)}, u32[]{:S(2)}) copy-start(f32[16]{0:T(128)} %get-tuple-element.31) | copy-start | bytes 196
  30.3 6.9 %copy-start.16 = (f32[2]{0:T(128)S(1)}, f32[2]{0:T(128)}, u32[]{:S(2)}) copy-start(f32[2]{0:T(128)} %compare_convert_fusion) | copy-start | bytes 28
  35.6 5.5 %slice-start.2 = ((s8[4423680]{0:T(1024)(128)(4,1)}), s8[4194304]{0:T(1024)(128)(4,1)S(1)}, s32[]{:S(2)}) async-start(s8[4423680]{0:T(1024)(128)(4,1)} %bitcast.47), calls=%async_computation.3 | async-start | bytes 8388608
  37.1 4.0 %slice-start.3 = ((s8[4423680]{0:T(1024)(128)(4,1)}), s8[229376]{0:T(1024)(128)(4,1)S(1)}, s32[]{:S(2)}) async-start(s8[4423680]{0:T(1024)(128)(4,1)} %bitcast.47), calls=%async_computation.4 | async-start | bytes 458752
  37.2 7.1 %slice-start = ((s8[4423680]{0:T(1024)(128)(4,1)}), s8[4194304]{0:T(1024)(128)(4,1)S(1)}, s32[]{:S(2)}) async-start(s8[4423680]{0:T(1024)(128)(4,1)} %bitcast.44), calls=%async_computation.1 | async-start | bytes 8388608
  54.1 16.0 %all-to-all-start = ((f32[16,2,1440]{2,1,0:T(2,128)}), f32[16,2,1440]{2,1,0:T(2,128)S(1)}, u32[]{:S(2)}, u32[]{:S(2)}) async-start(f32[16,2,1440]{2,1,0:T(2,128)} %broadcast_select_fusion), calls=%async_computation | async-start | bytes 393216 | tf_op jit(solution)/shard_map/all_to_all | solution.py:129
  (5 other events, 12.2 us)

commit v2 on v1

v2 whole, which is shorter than its diff:
```python
import functools
import math

import jax
import jax.numpy as jnp
import numpy as np
from jax import lax
from jax.experimental import pallas as pl
from jax.experimental.pallas import tpu as pltpu
from jax.sharding import PartitionSpec as P

SLOT_DEV = 9
CHUNK = 256
PI = math.pi
COS_CUT = math.cos(40.0 * math.pi / 180.0)
F32 = jnp.float32
BF16 = jnp.bfloat16


def wave_numbers(nlon):
    ids = np.arange(nlon)
    return ids, np.where(ids <= nlon // 2, ids, ids - nlon // 2)


def spectral_table(nlon, padded):
    ids, wave = wave_numbers(nlon)
    angles = (ids[:, None] * wave[None, :] % nlon) * (2.0 * PI / nlon)
    edge = (ids == 0) | (ids == nlon // 2)
    weights = np.where(edge, math.sqrt(1.0 / nlon), math.sqrt(2.0 / nlon))
    table = np.where(ids[None, :] <= nlon // 2, np.cos(angles), np.sin(angles)) * weights[None, :]
    full = np.zeros((padded, padded), np.float32)
    full[:nlon, :nlon] = table
    high = full.astype(BF16)
    low = (full - high.astype(np.float32)).astype(BF16)
    return high, low


def sine_rows(nlon, padded):
    sines = np.ones((8, padded), np.float32)
    sines[:, :nlon] = np.abs(np.sin(wave_numbers(nlon)[1] * (PI / nlon)))
    return sines


def row_constants(total_rows):
    rows = np.arange(total_rows)
    cosine = np.cos((rows + 0.5) * (PI / total_rows) - 0.5 * PI)
    face = np.where(rows + 1 < total_rows, np.sin((rows + 1) * (PI / total_rows)), 0.0)
    before = np.where(rows > 0, np.sin(rows * (PI / total_rows)), 0.0)
    out = np.zeros((total_rows, 128), np.float32)
    out[:, 0] = cosine / COS_CUT
    out[:, 1] = face / cosine
    out[:, 2] = before / cosine
    return out


def next_lane(x):
    return jnp.concatenate([x[:, 1:], x[:, :1]], axis=1)


def prev_lane(x):
    return jnp.concatenate([x[:, -1:], x[:, :-1]], axis=1)


def pos(x):
    return jnp.maximum(x, 0.0)


def neg(x):
    return jnp.minimum(x, 0.0)


def kernel(
    lat_count, lev_count, cap,
    th_in, tr_in, east_in, north_in, vert_in, flags, slots, slots_row, high_in, low_in, rowc_in, sines,
    th_out, tr_out, spectra,
    th, tr, vert, east, north, high, low, rowc,
    up_buf, down_buf, from_south, from_north,
    damp, change, left, mid, res, coef0, packed, arrived, out_buf,
    in_sems, lev_send, lev_recv, lat_send, lat_recv, sp_send, sp_recv, self_sems, out_sems,
):
    fields = tr_in.shape[0] + 1
    rows_dev, nlon = th_in.shape[1], th_in.shape[2]
    padded = high.shape[0]
    count = fields * rows_dev
    band = lax.axis_index("lat")
    lev = lax.axis_index("lev")

    loads = [
        pltpu.make_async_copy(th_in, th.at[pl.ds(1, 2)], in_sems.at[0]),
        pltpu.make_async_copy(tr_in, tr.at[:, pl.ds(1, 2)], in_sems.at[1]),
        pltpu.make_async_copy(north_in, north, in_sems.at[2]),
        pltpu.make_async_copy(vert_in, vert.at[pl.ds(1, 2)], in_sems.at[3]),
        pltpu.make_async_copy(east_in, east, in_sems.at[4]),
        pltpu.make_async_copy(rowc_in.at[pl.ds(band * rows_dev, rows_dev)], rowc, in_sems.at[5]),
        pltpu.make_async_copy(high_in, high, in_sems.at[6]),
        pltpu.make_async_copy(low_in, low, in_sems.at[7]),
    ]
    for load in loads[:6]:
        load.start()

    barrier = pltpu.get_barrier_semaphore()

    def greet(peer):
        pl.semaphore_signal(barrier, inc=1, device_id=peer, device_id_type=pl.DeviceIdType.MESH)

    for k in range(1, lat_count):
        greet((lax.rem(band + k, lat_count), lev))

    @pl.when(lev > 0)
    def _():
        greet((band, lev - 1))

    @pl.when(lev < lev_count - 1)
    def _():
        greet((band, lev + 1))

    beside = jnp.where(lev > 0, 1, 0) + jnp.where(lev < lev_count - 1, 1, 0)
    pl.semaphore_wait(barrier, lat_count - 1 + beside)

    def remote(src, dst, send, recv, peer):
        return pltpu.make_async_remote_copy(
            src_ref=src, dst_ref=dst, send_sem=send, recv_sem=recv,
            device_id=peer, device_id_type=pl.DeviceIdType.MESH,
        )

    down = (band, lev + 1)
    up = (band, lev - 1)
    to_next = [
        remote(th_in.at[1], th.at[0], lev_send.at[0], lev_recv.at[0], down),
        remote(vert_in.at[1], vert.at[0], lev_send.at[1], lev_recv.at[1], down),
        remote(tr_in.at[:, 1], tr.at[:, 0], lev_send.at[2], lev_recv.at[2], down),
    ]
    to_prev = [
        remote(th_in.at[0], th.at[3], lev_send.at[3], lev_recv.at[3], up),
        remote(tr_in.at[:, 0], tr.at[:, 3], lev_send.at[4], lev_recv.at[4], up),
    ]

    @pl.when(lev < lev_count - 1)
    def _():
        for copy in to_next:
            copy.start()

    @pl.when(lev > 0)
    def _():
        for copy in to_prev:
            copy.start()

    for load in loads[6:]:
        load.start()

    @pl.when(lev == 0)
    def _():
        th[0] = jnp.zeros_like(th[0])
        vert[0] = jnp.zeros_like(vert[0])
        tr[:, 0] = jnp.zeros_like(tr[:, 0])

    @pl.when(lev == lev_count - 1)
    def _():
        th[3] = jnp.zeros_like(th[3])
        tr[:, 3] = jnp.zeros_like(tr[:, 3])

    for load in loads[:3]:
        load.wait()
    up_buf[...] = jnp.zeros_like(up_buf)
    down_buf[...] = jnp.zeros_like(down_buf)
    for l in range(2):
        for buf, at in ((up_buf, rows_dev - 1), (down_buf, 0)):
            base = th[l + 1, at : at + 1, :]
            buf[l, 0:1, :] = base
            for f in range(1, fields):
                buf[l, f : f + 1, :] = base * tr[f - 1, l + 1, at : at + 1, :]
        up_buf[l, fields : fields + 1, :] = north[l, rows_dev - 1 : rows_dev, :]
    to_north = remote(up_buf, from_south, lat_send.at[0], lat_recv.at[0], (band + 1, lev))
    to_south = remote(down_buf, from_north, lat_send.at[1], lat_recv.at[1], (band - 1, lev))

    @pl.when(band < lat_count - 1)
    def _():
        to_north.start()

    @pl.when(band > 0)
    def _():
        to_south.start()

    @pl.when(band == 0)
    def _():
        from_south[...] = jnp.zeros_like(from_south)

    @pl.when(band == lat_count - 1)
    def _():
        from_north[...] = jnp.zeros_like(from_north)

    for load in loads[3:6]:
        load.wait()
    ratio = rowc[:, 0:1]
    fraction = ratio / jnp.maximum(ratio, sines[0:1, :])
    damp[...] = fraction * fraction
    left[:, nlon:] = jnp.zeros((2 * count, padded - nlon), BF16)

    row_iota = lax.broadcasted_iota(jnp.int32, (rows_dev, 1), 0)
    owners, keys = [], []
    flag_col = jnp.zeros((rows_dev, 1), jnp.int32)
    for j in range(rows_dev):
        flag = flags[band * rows_dev + j]
        slot = slots[band * rows_dev + j]
        owner = jnp.where((flag == 1) & (slot >= 0), lax.div(jnp.maximum(slot, 0), SLOT_DEV), -1)
        rank = jnp.int32(0)
        for other in owners:
            rank = rank + jnp.where(other == owner, 1, 0)
        owners.append(owner)
        keys.append(jnp.where(owner >= 0, owner * cap + rank, -1))
        flag_col = jnp.where(row_iota == j, flag, flag_col)
    flagged = flag_col == 1
    picks = []
    for q in range(lat_count * cap):
        pick = jnp.int32(0)
        for j in range(rows_dev):
            pick = jnp.where(keys[j] == q, j, pick)
        picks.append(pick)

    row = slots_row[...]
    total = row.shape[1]
    slot_rows = 16
    lane = lax.broadcasted_iota(jnp.int32, (slot_rows, total), 1)
    place = lax.broadcasted_iota(jnp.int32, (slot_rows, total), 0)
    first = band * SLOT_DEV
    shift = rows_dev.bit_length() - 1
    full = jnp.broadcast_to(row, (slot_rows, total))
    hit = (full == first + place) & (place < SLOT_DEV)
    source_row = jnp.sum(jnp.where(hit, lane, 0).astype(F32), axis=1, keepdims=True).astype(jnp.int32)
    source = lax.shift_right_logical(source_row, shift)
    mine = (full >= first) & (full < first + SLOT_DEV)
    before = mine & (lax.shift_right_logical(lane, shift) == source) & (lane < source_row)
    ranks = jnp.sum(jnp.where(before, 1.0, 0.0), axis=1, keepdims=True).astype(jnp.int32)
    arrival = source * cap + ranks

    @pl.when(band < lat_count - 1)
    def _():
        to_south.wait_recv()

    @pl.when(band > 0)
    def _():
        to_north.wait_recv()

    def spectra_copy(l, k):
        peer = lax.rem(band + k, lat_count)
        return remote(
            packed.at[l, peer], arrived.at[l, band], sp_send.at[l, peer], sp_recv.at[l, band], (peer, lev)
        )

    def spectra_arrival(l, k):
        peer = lax.rem(band + k, lat_count)
        return remote(
            packed.at[l, peer], arrived.at[l, peer], sp_send.at[l, peer], sp_recv.at[l, peer], (peer, lev)
        )

    def own_copy(l):
        return pltpu.make_async_copy(packed.at[l, band], arrived.at[l, band], self_sems.at[l])

    def out_copies(l):
        return [
            pltpu.make_async_copy(out_buf.at[l, 0], th_out.at[l], out_sems.at[l, 0]),
            pltpu.make_async_copy(out_buf.at[l, pl.ds(1, fields - 1)], tr_out.at[:, l], out_sems.at[l, 1]),
        ]

    def product(ref, table, at, across):
        part = pl.ds(at * CHUNK, CHUNK)
        dims = (((1,), (1,)), ((), ())) if across else (((1,), (0,)), ((), ()))
        pick = (lambda t: t[part, :]) if across else (lambda t: t[:, part])
        both = lax.dot_general(ref[...], pick(high), dims, preferred_element_type=F32)
        rest = lax.dot_general(ref[0:count, :], pick(low), dims, preferred_element_type=F32)
        return both[:count] + (both[count:] + rest)

    def split_to(ref, at, cols, x):
        n = x.shape[0]
        hi = x.astype(BF16)
        ref[at : at + n, cols] = hi
        ref[count + at : count + at + n, cols] = (x - hi.astype(F32)).astype(BF16)

    def level(t, carry):
        even = lax.rem(lev, 2)
        l = jnp.where(t == 0, 1 - even, even)

        @pl.when((l == 0) & (lev > 0))
        def _():
            for copy in to_next:
                copy.wait_recv()

        @pl.when((l == 1) & (lev < lev_count - 1))
        def _():
            for copy in to_prev:
                copy.wait_recv()

        inner = jnp.where(lev * 2 + l + 1 < lev_count * 2, 1.0, 0.0).astype(F32)
        e = east[l]
        ew = prev_lane(e)
        n = north[l]
        ns = jnp.concatenate([from_south[l, fields : fields + 1, :], n[:-1, :]], axis=0)
        v = vert[l + 1] * inner
        va = vert[l]
        fn = rowc[:, 1:2]
        fs = rowc[:, 2:3]
        centre = pos(e) - neg(ew) + fn * pos(n) - fs * neg(ns) + (pos(v) - neg(va))
        c_e, c_w = neg(e), pos(ew)
        c_n, c_s = fn * neg(n), fs * pos(ns)
        c_b, c_a = neg(v), pos(va)
        for f in range(fields):
            if f == 0:
                x, above, below = th[l + 1], th[l], th[l + 2]
            else:
                x = th[l + 1] * tr[f - 1, l + 1]
                above = th[l] * tr[f - 1, l]
                below = th[l + 2] * tr[f - 1, l + 2]
            x_n = jnp.concatenate([x[1:, :], from_north[l, f : f + 1, :]], axis=0)
            x_s = jnp.concatenate([from_south[l, f : f + 1, :], x[:-1, :]], axis=0)
            tend = (c_w * prev_lane(x) - c_e * next_lane(x)) + (c_s * x_s - c_n * x_n)
            tend = tend + (c_a * above - c_b * below) - centre * x
            change[f * rows_dev : (f + 1) * rows_dev, :] = tend
            out_buf[l, f] = x
            split_to(left, f * rows_dev, slice(0, nlon), tend)

        @pl.when(t == 0)
        def _():
            for load in loads[6:]:
                load.wait()

        for at in range(padded // CHUNK):
            cols = slice(at * CHUNK, (at + 1) * CHUNK)
            coef = product(left, high, at, False).reshape(fields, rows_dev, CHUNK)
            coef = (coef * damp[:, cols][None]).reshape(count, CHUNK)
            coef0[:, cols] = coef[:rows_dev]
            split_to(mid, 0, cols, coef)
        for q in range(lat_count * cap):
            packed[l, q // cap, q % cap : q % cap + 1, :] = coef0[pl.ds(picks[q], 1), :][:, :nlon]
        own_copy(l).start()
        for k in range(1, lat_count):
            spectra_copy(l, k).start()
        for at in range(padded // CHUNK):
            cols = slice(at * CHUNK, (at + 1) * CHUNK)
            res[:, cols] = product(mid, high, at, True)
        for f in range(fields):
            part = slice(f * rows_dev, (f + 1) * rows_dev)
            out_buf[l, f] = out_buf[l, f] + jnp.where(flagged, res[part, :nlon], change[part, :])
        for copy in out_copies(l):
            copy.start()
        return carry

    lax.fori_loop(0, 2, level, 0)

    for l in range(2):
        own_copy(l).wait()
        for k in range(1, lat_count):
            spectra_arrival(l, k).wait_recv()
        value = jnp.zeros((slot_rows, nlon), F32)
        for q in range(lat_count * cap):
            value = jnp.where(arrival == q, arrived[l, q // cap, q % cap : q % cap + 1, :], value)
        for p in range(SLOT_DEV):
            spectra[p, l : l + 1, :] = value[p : p + 1, :]
        for k in range(1, lat_count):
            spectra_copy(l, k).wait_send()

    @pl.when(lev < lev_count - 1)
    def _():
        for copy in to_next:
            copy.wait_send()

    @pl.when(lev > 0)
    def _():
        for copy in to_prev:
            copy.wait_send()

    @pl.when(band < lat_count - 1)
    def _():
        to_north.wait_send()

    @pl.when(band > 0)
    def _():
        to_south.wait_send()

    for l in range(2):
        for copy in out_copies(l):
            copy.wait()


def local(thickness, tracers, east, north, vert, flags, slots, high, low, rowc, sines):
    lat_count = lax.axis_size("lat")
    lev_count = lax.axis_size("lev")
    lev_dev, rows_dev, nlon = thickness.shape
    padded = high.shape[0]
    fields = tracers.shape[0] + 1
    count = fields * rows_dev
    cap = -(-rows_dev // lat_count)
    anywhere = pl.BlockSpec(memory_space=pl.ANY)
    vmem = pl.BlockSpec(memory_space=pltpu.VMEM)
    smem = pl.BlockSpec(memory_space=pltpu.SMEM)
    dma = pltpu.SemaphoreType.DMA
    return pl.pallas_call(
        functools.partial(kernel, lat_count, lev_count, cap),
        out_shape=(
            jax.ShapeDtypeStruct(thickness.shape, F32),
            jax.ShapeDtypeStruct(tracers.shape, F32),
            jax.ShapeDtypeStruct((SLOT_DEV, lev_dev, nlon), F32),
        ),
        in_specs=[anywhere] * 5 + [smem, smem, vmem] + [anywhere] * 3 + [vmem],
        out_specs=(anywhere, anywhere, vmem),
        scratch_shapes=[
            pltpu.VMEM((4, rows_dev, nlon), F32),
            pltpu.VMEM((fields - 1, 4, rows_dev, nlon), F32),
            pltpu.VMEM((3, rows_dev, nlon), F32),
            pltpu.VMEM((2, rows_dev, nlon), F32),
            pltpu.VMEM((2, rows_dev, nlon), F32),
            pltpu.VMEM((padded, padded), BF16),
            pltpu.VMEM((padded, padded), BF16),
            pltpu.VMEM((rows_dev, 128), F32),
            pltpu.VMEM((2, 16, nlon), F32),
            pltpu.VMEM((2, 16, nlon), F32),
            pltpu.VMEM((2, 16, nlon), F32),
            pltpu.VMEM((2, 16, nlon), F32),
            pltpu.VMEM((rows_dev, padded), F32),
            pltpu.VMEM((count, nlon), F32),
            pltpu.VMEM((2 * count, padded), BF16),
            pltpu.VMEM((2 * count, padded), BF16),
            pltpu.VMEM((count, padded), F32),
            pltpu.VMEM((rows_dev, padded), F32),
            pltpu.VMEM((2, lat_count, cap, nlon), F32),
            pltpu.VMEM((2, lat_count, cap, nlon), F32),
            pltpu.VMEM((2, fields, rows_dev, nlon), F32),
            dma((8,)),
            dma((5,)),
            dma((5,)),
            dma((2,)),
            dma((2,)),
            dma((2, lat_count)),
            dma((2, lat_count)),
            dma((2,)),
            dma((2, 2)),
        ],
        compiler_params=pltpu.CompilerParams(
            collective_id=0, has_side_effects=True, vmem_limit_bytes=48 * 1024 * 1024
        ),
    )(thickness, tracers, east, north, vert, flags, slots, slots.reshape(1, -1), high, low, rowc, sines)


def solution(mesh):
    def run(thickness, tracers, east, north, vert, flags, slots):
        total_rows, nlon = thickness.shape[1:]
        padded = -(-nlon // CHUNK) * CHUNK
        high, low = spectral_table(nlon, padded)
        cells = P("lev", "lat", None)
        mapped = jax.shard_map(
            local,
            mesh=mesh,
            in_specs=(cells, P(None, "lev", "lat", None), cells, cells, cells) + (P(),) * 6,
            out_specs=(cells, P(None, "lev", "lat", None), P("lat", "lev", None)),
            check_vma=False,
        )
        tables = (high, low, row_constants(total_rows), sine_rows(nlon, padded))
        return mapped(
            thickness, tracers, east, north, vert, flags, slots, *(jnp.asarray(t) for t in tables)
        )

    return run
```

time: 72 us -> 42.7 us (0.59)
  Pallas kernels: 0 us -> 31.2 us
  other arithmetic: 25.1 us -> 0 us
  starting transfers between devices: 17.7 us -> 0 us
  matrix products: 9.77 us -> 0 us
  waiting for transfers between devices: 8.33 us -> 0 us
  local copies, waits for them, and re-layouts: 9.43 us -> 10.5 us
    pallas_call x0 -> x1, Pallas kernels: none -> 31.2 us  [local(): pl.pallas_call(functools.partial(kernel, lat_count, lev_count, cap), out_...]
    ppermute x4 -> x0, starting transfers between devices: 10.8 us -> none  [shifted(): return lax.ppermute(x, axis, pairs)]
    unnamed x48 -> x21, local copies, waits for them, and re-layouts: 0.11 us -> 10.5 us
    dot_general x6 -> x0, matrix products: 9.77 us -> none  [product(): lax.dot_general(a, b, dims, preferred_element_type=jnp.float32)]
    all_to_all x1 -> x0, waiting for transfers between devices: 8.32 us -> none  [local(): lax.all_to_all(outgoing, 'lat', split_axis=0, concat_axis=0, tiled=True)]
    concatenate x7 -> x0, other arithmetic: 8.22 us -> none  [the longest x5 6.44 us: local(): jnp.concatenate([thickness[None], thickness[None] * tracers], axis=0)]
    all_to_all x1 -> x0, starting transfers between devices: 6.95 us -> none  [local(): lax.all_to_all(outgoing, 'lat', split_axis=0, concat_axis=0, tiled=True)]
    slice x5 -> x0, local copies, waits for them, and re-layouts: 5.42 us -> none  [the longest x1 1.6 us: local(): above_courant = jnp.concatenate([from_above[-1], vert_courant[:-1]], axis=0)]
  transfers between devices with their start and end apart: 5 -> 0, of which waited for: 1 -> 0; matrix products, arithmetic and copies ran while one was open for 29% -> 0% of each run, Pallas kernels for 0% -> 0%
where the time goes in v2:
time: 42.7 us; the launch traced here: 42.3 us
  Pallas kernels  31.2 us (73%)
  local copies, waits for them, and re-layouts  10.5 us (25%)
  between operations  0.66 us (2%)
    pallas_call x1, Pallas kernels, local(): pl.pallas_call(functools.partial(kernel, lat_count, lev_count, cap), out_...  31.2 us
    unnamed x21, local copies, waits for them, and re-layouts  10.5 us

profile of v2, /device:TPU:0, one launch (start us, length us, event | category | flops | bytes accessed | tf_op | source)
XLA Modules:
  0.0 42.3 jit_solution(15865240743116868646)
XLA Ops:
  0.6 0.0 copy-start
  0.6 1.4 %copy-done = f32[8,2,16,1440]{3,2,1,0:T(8,128)S(1)} copy-done((f32[8,2,16,1440]{3,2,1,0:T(8,128)S(1)}, f32[8,2,16,1440]{3,2,1,0:T(8,128)}, u32[]{:S(2)}) %copy-start) | copy-done | bytes 1474584
  2.0 0.0 copy-start.1
  2.0 0.9 %copy-done.1 = f32[2,16,1440]{2,1,0:T(8,128)S(1)} copy-done((f32[2,16,1440]{2,1,0:T(8,128)S(1)}, f32[2,16,1440]{2,1,0:T(8,128)}, u32[]{:S(2)}) %copy-start.1) | copy-done | bytes 184344
  3.0 0.0 copy-start.2
  3.0 0.9 %copy-done.2 = f32[2,16,1440]{2,1,0:T(8,128)S(1)} copy-done((f32[2,16,1440]{2,1,0:T(8,128)S(1)}, f32[2,16,1440]{2,1,0:T(8,128)}, u32[]{:S(2)}) %copy-start.2) | copy-done | bytes 184344
  3.9 0.0 copy-start.3
  3.9 0.9 %copy-done.3 = f32[2,16,1440]{2,1,0:T(8,128)S(1)} copy-done((f32[2,16,1440]{2,1,0:T(8,128)S(1)}, f32[2,16,1440]{2,1,0:T(8,128)}, u32[]{:S(2)}) %copy-start.3) | copy-done | bytes 184344
  4.8 0.0 copy-start.4
  4.8 0.9 %copy-done.4 = f32[2,16,1440]{2,1,0:T(8,128)S(1)} copy-done((f32[2,16,1440]{2,1,0:T(8,128)S(1)}, f32[2,16,1440]{2,1,0:T(8,128)}, u32[]{:S(2)}) %copy-start.4) | copy-done | bytes 184344
  5.8 0.0 copy-start.5
  5.8 0.8 %copy-done.5 = f32[128,128]{1,0:T(8,128)S(1)} copy-done((f32[128,128]{1,0:T(8,128)S(1)}, f32[128,128]{1,0:T(8,128)}, u32[]{:S(2)}) %copy-start.5) | copy-done | bytes 65560
  6.6 0.0 copy-start.6
  6.6 0.8 %copy-done.6 = f32[8,1536]{1,0:T(8,128)S(1)} copy-done((f32[8,1536]{1,0:T(8,128)S(1)}, f32[8,1536]{1,0:T(8,128)}, u32[]{:S(2)}) %copy-start.6) | copy-done | bytes 49176
  7.4 0.0 copy-start.7
  7.4 0.7 %copy-done.7 = s32[128]{0:T(128)S(1)} copy-done((s32[128]{0:T(128)S(1)}, s32[128]{0:T(128)}, u32[]{:S(2)}) %copy-start.7) | copy-done | bytes 536
  8.0 0.0 copy-start.8
  8.0 0.7 %copy-done.8 = s32[128]{0:T(128)S(1)} copy-done((s32[128]{0:T(128)S(1)}, s32[128]{0:T(128)}, u32[]{:S(2)}) %copy-start.8) | copy-done | bytes 536
  8.7 31.2 %shard_map.130 = (f32[2,16,1440]{2,1,0:T(8,128)S(1)}, f32[8,2,16,1440]{3,2,1,0:T(8,128)S(1)}, f32[9,2,1440]{2,1,0:T(2,128)S(1)}) custom-call(f32[2,16,1440]{2,1,0:T(8,128)S(1)} %copy-done.1, f32[8,2,16,1440]{3,2,1,0:T(8,128)S(1)} %copy-done, f32[2,16,1440]{2,1,0:T(8,128)S(1)} %copy-done.2, f32[2,16,1440]{2,1,0:T(8,128)S(1)} %copy-done.3, ...), custom_call_target="tpu_custom_call" | custom-call | tf_op jit(solution)/shard_map/pallas_call | solution.py:396
  39.9 0.7 %copy.17 = f32[2,16,1440]{2,1,0:T(8,128)} copy(f32[2,16,1440]{2,1,0:T(8,128)S(1)} %get-tuple-element.6) | data formatting | bytes 368640
  40.6 1.1 %copy.18 = f32[8,2,16,1440]{3,2,1,0:T(8,128)} copy(f32[8,2,16,1440]{3,2,1,0:T(8,128)S(1)} %get-tuple-element.7) | data formatting | bytes 2949120
  41.7 0.6 %copy.19 = f32[9,2,1440]{2,1,0:T(2,128)} copy(f32[9,2,1440]{2,1,0:T(2,128)S(1)} %get-tuple-element.8) | data formatting | bytes 207360
Async XLA Ops:
  0.6 1.4 %copy-start = (f32[8,2,16,1440]{3,2,1,0:T(8,128)S(1)}, f32[8,2,16,1440]{3,2,1,0:T(8,128)}, u32[]{:S(2)}) copy-start(f32[8,2,16,1440]{3,2,1,0:T(8,128)} %tr_in.1) | copy-start | bytes 4423684
  2.0 0.9 %copy-start.1 = (f32[2,16,1440]{2,1,0:T(8,128)S(1)}, f32[2,16,1440]{2,1,0:T(8,128)}, u32[]{:S(2)}) copy-start(f32[2,16,1440]{2,1,0:T(8,128)} %th_in.1) | copy-start | bytes 552964
  3.0 0.9 %copy-start.2 = (f32[2,16,1440]{2,1,0:T(8,128)S(1)}, f32[2,16,1440]{2,1,0:T(8,128)}, u32[]{:S(2)}) copy-start(f32[2,16,1440]{2,1,0:T(8,128)} %east_in.1) | copy-start | bytes 552964
  3.9 0.9 %copy-start.3 = (f32[2,16,1440]{2,1,0:T(8,128)S(1)}, f32[2,16,1440]{2,1,0:T(8,128)}, u32[]{:S(2)}) copy-start(f32[2,16,1440]{2,1,0:T(8,128)} %north_in.1) | copy-start | bytes 552964
  4.8 0.9 %copy-start.4 = (f32[2,16,1440]{2,1,0:T(8,128)S(1)}, f32[2,16,1440]{2,1,0:T(8,128)}, u32[]{:S(2)}) copy-start(f32[2,16,1440]{2,1,0:T(8,128)} %vert_in.1) | copy-start | bytes 552964
  5.8 0.8 %copy-start.5 = (f32[128,128]{1,0:T(8,128)S(1)}, f32[128,128]{1,0:T(8,128)}, u32[]{:S(2)}) copy-start(f32[128,128]{1,0:T(8,128)} %constant.10.clone.rowc_in) | copy-start | bytes 196612
  6.6 0.8 %copy-start.6 = (f32[8,1536]{1,0:T(8,128)S(1)}, f32[8,1536]{1,0:T(8,128)}, u32[]{:S(2)}) copy-start(f32[8,1536]{1,0:T(8,128)} %constant.11.clone.sines) | copy-start | bytes 147460
  7.4 0.7 %copy-start.7 = (s32[128]{0:T(128)S(1)}, s32[128]{0:T(128)}, u32[]{:S(2)}) copy-start(s32[128]{0:T(128)} %slots.1) | copy-start | bytes 1540
  8.0 0.7 %copy-start.8 = (s32[128]{0:T(128)S(1)}, s32[128]{0:T(128)}, u32[]{:S(2)}) copy-start(s32[128]{0:T(128)} %flags.1) | copy-start | bytes 1540

commit v3 on v2

--- a/solution.py
+++ b/solution.py
@@ -17,28 +17,42 @@
 BF16 = jnp.bfloat16
 
 
-def wave_numbers(nlon):
-    ids = np.arange(nlon)
-    return ids, np.where(ids <= nlon // 2, ids, ids - nlon // 2)
-
-
-def spectral_table(nlon, padded):
-    ids, wave = wave_numbers(nlon)
-    angles = (ids[:, None] * wave[None, :] % nlon) * (2.0 * PI / nlon)
-    edge = (ids == 0) | (ids == nlon // 2)
-    weights = np.where(edge, math.sqrt(1.0 / nlon), math.sqrt(2.0 / nlon))
-    table = np.where(ids[None, :] <= nlon // 2, np.cos(angles), np.sin(angles)) * weights[None, :]
-    full = np.zeros((padded, padded), np.float32)
-    full[:nlon, :nlon] = table
+def columns(nlon):
+    half, quarter = nlon // 2, nlon // 4
+    part = -(-(quarter + 1) // 128) * 128
+    waves = np.full((2, 2, part), -1)
+    waves[0, 0, : quarter + 1] = 2 * np.arange(quarter + 1)
+    waves[0, 1, 1:quarter] = 2 * np.arange(1, quarter)
+    waves[1, :, :quarter] = 2 * np.arange(quarter) + 1
+    return half, part, waves
+
+
+def spectral_table(nlon):
+    half, part, waves = columns(nlon)
+    full = np.zeros((2, 2 * part, 2, part), np.float32)
+    angles = (np.arange(half)[:, None, None, None] * waves[None] % nlon) * (2.0 * PI / nlon)
+    edge = (waves == 0) | (waves == half)
+    weights = np.where(edge, math.sqrt(1.0 / nlon), math.sqrt(2.0 / nlon)) * (waves >= 0)
+    table = np.stack([np.cos(angles[:, :, 0]), np.sin(angles[:, :, 1])], axis=2) * weights[None]
+    full[:, :half] = np.moveaxis(table, 1, 0)
+    full = full.reshape(2, 2 * part, 2 * part)
     high = full.astype(BF16)
     low = (full - high.astype(np.float32)).astype(BF16)
     return high, low
 
 
-def sine_rows(nlon, padded):
-    sines = np.ones((8, padded), np.float32)
-    sines[:, :nlon] = np.abs(np.sin(wave_numbers(nlon)[1] * (PI / nlon)))
-    return sines
+def sine_rows(nlon):
+    _, _, waves = columns(nlon)
+    sines = np.where(waves >= 0, np.abs(np.sin(waves * (PI / nlon))), 1.0).reshape(1, -1)
+    return np.broadcast_to(sines, (8, sines.shape[1])).astype(np.float32)
+
+
+def interleave():
+    out = np.zeros((CHUNK, CHUNK), np.float32)
+    ids = np.arange(CHUNK // 2)
+    out[ids, 2 * ids] = 1.0
+    out[CHUNK // 2 + ids, 2 * ids + 1] = 1.0
+    return out.astype(BF16)
 
 
 def row_constants(total_rows):
@@ -71,16 +85,16 @@
 
 def kernel(
     lat_count, lev_count, cap,
-    th_in, tr_in, east_in, north_in, vert_in, flags, slots, slots_row, high_in, low_in, rowc_in, sines,
+    th_in, tr_in, east_in, north_in, vert_in, flags_in, slots_in, row_in, high_in, low_in, rowc_in, sines_in, weave_in,
     th_out, tr_out, spectra,
-    th, tr, vert, east, north, high, low, rowc,
+    th, tr, vert, east, north, high, low, rowc, sines, weave, slots_row, flags, slots,
     up_buf, down_buf, from_south, from_north,
     damp, change, left, mid, res, coef0, packed, arrived, out_buf,
     in_sems, lev_send, lev_recv, lat_send, lat_recv, sp_send, sp_recv, self_sems, out_sems,
 ):
     fields = tr_in.shape[0] + 1
     rows_dev, nlon = th_in.shape[1], th_in.shape[2]
-    padded = high.shape[0]
+    half, padded = nlon // 2, high.shape[1]
     count = fields * rows_dev
     band = lax.axis_index("lat")
     lev = lax.axis_index("lev")
@@ -92,10 +106,15 @@
         pltpu.make_async_copy(vert_in, vert.at[pl.ds(1, 2)], in_sems.at[3]),
         pltpu.make_async_copy(east_in, east, in_sems.at[4]),
         pltpu.make_async_copy(rowc_in.at[pl.ds(band * rows_dev, rows_dev)], rowc, in_sems.at[5]),
-        pltpu.make_async_copy(high_in, high, in_sems.at[6]),
-        pltpu.make_async_copy(low_in, low, in_sems.at[7]),
+        pltpu.make_async_copy(sines_in, sines, in_sems.at[6]),
+        pltpu.make_async_copy(row_in, slots_row, in_sems.at[7]),
+        pltpu.make_async_copy(flags_in, flags, in_sems.at[8]),
+        pltpu.make_async_copy(slots_in, slots, in_sems.at[9]),
+        pltpu.make_async_copy(high_in, high, in_sems.at[10]),
+        pltpu.make_async_copy(low_in, low, in_sems.at[11]),
+        pltpu.make_async_copy(weave_in, weave, in_sems.at[12]),
     ]
-    for load in loads[:6]:
+    for load in loads[:10]:
         load.start()
 
     barrier = pltpu.get_barrier_semaphore()
@@ -145,7 +164,7 @@
         for copy in to_prev:
             copy.start()
 
-    for load in loads[6:]:
+    for load in loads[10:]:
         load.start()
 
     @pl.when(lev == 0)
@@ -189,12 +208,12 @@
     def _():
         from_north[...] = jnp.zeros_like(from_north)
 
-    for load in loads[3:6]:
+    for load in loads[3:10]:
         load.wait()
     ratio = rowc[:, 0:1]
     fraction = ratio / jnp.maximum(ratio, sines[0:1, :])
     damp[...] = fraction * fraction
-    left[:, nlon:] = jnp.zeros((2 * count, padded - nlon), BF16)
+    left[:, :, half:] = jnp.zeros((2, 2 * count, padded - half), BF16)
 
     row_iota = lax.broadcasted_iota(jnp.int32, (rows_dev, 1), 0)
     owners, keys = [], []
@@ -262,19 +281,19 @@
             pltpu.make_async_copy(out_buf.at[l, pl.ds(1, fields - 1)], tr_out.at[:, l], out_sems.at[l, 1]),
         ]
 
-    def product(ref, table, at, across):
+    def product(ref, side, at, across):
         part = pl.ds(at * CHUNK, CHUNK)
         dims = (((1,), (1,)), ((), ())) if across else (((1,), (0,)), ((), ()))
-        pick = (lambda t: t[part, :]) if across else (lambda t: t[:, part])
-        both = lax.dot_general(ref[...], pick(high), dims, preferred_element_type=F32)
-        rest = lax.dot_general(ref[0:count, :], pick(low), dims, preferred_element_type=F32)
+        pick = (lambda t: t[side, part, :]) if across else (lambda t: t[side, :, part])
+        both = lax.dot_general(ref[side], pick(high), dims, preferred_element_type=F32)
+        rest = lax.dot_general(ref[side, 0:count, :], pick(low), dims, preferred_element_type=F32)
         return both[:count] + (both[count:] + rest)
 
-    def split_to(ref, at, cols, x):
+    def split_to(ref, side, at, cols, x):
         n = x.shape[0]
         hi = x.astype(BF16)
-        ref[at : at + n, cols] = hi
-        ref[count + at : count + at + n, cols] = (x - hi.astype(F32)).astype(BF16)
+        ref[side, at : at + n, cols] = hi
+        ref[side, count + at : count + at + n, cols] = (x - hi.astype(F32)).astype(BF16)
 
     def level(t, carry):
         even = lax.rem(lev, 2)
@@ -316,30 +335,44 @@
             tend = tend + (c_a * above - c_b * below) - centre * x
             change[f * rows_dev : (f + 1) * rows_dev, :] = tend
             out_buf[l, f] = x
-            split_to(left, f * rows_dev, slice(0, nlon), tend)
+            split_to(left, 0, f * rows_dev, slice(0, half), tend[:, :half] + tend[:, half:])
+            split_to(left, 1, f * rows_dev, slice(0, half), tend[:, :half] - tend[:, half:])
 
         @pl.when(t == 0)
         def _():
-            for load in loads[6:]:
+            for load in loads[10:]:
                 load.wait()
 
-        for at in range(padded // CHUNK):
-            cols = slice(at * CHUNK, (at + 1) * CHUNK)
-            coef = product(left, high, at, False).reshape(fields, rows_dev, CHUNK)
-            coef = (coef * damp[:, cols][None]).reshape(count, CHUNK)
-            coef0[:, cols] = coef[:rows_dev]
-            split_to(mid, 0, cols, coef)
+        for side in range(2):
+            for at in range(padded // CHUNK):
+                cols = slice(at * CHUNK, (at + 1) * CHUNK)
+                coef = product(left, side, at, False).reshape(fields, rows_dev, CHUNK)
+                coef = coef * damp[:, side * padded + at * CHUNK : side * padded + (at + 1) * CHUNK][None]
+                split_to(mid, side, 0, cols, coef.reshape(count, CHUNK))
+        lanes = CHUNK // 2
+        rows_of = (slice(0, rows_dev), slice(count, count + rows_dev))
+        pieces = []
+        for at in range(padded // lanes):
+            cols = slice(at * lanes, (at + 1) * lanes)
+            pairs = [jnp.concatenate([mid[0, r, cols], mid[1, r, cols]], axis=1) for r in rows_of]
+            both = jnp.dot(jnp.concatenate(pairs, axis=0), weave[...], preferred_element_type=F32)
+            pieces.append(both[:rows_dev] + both[rows_dev:])
+        cosines = jnp.concatenate(pieces[: len(pieces) // 2], axis=1)
+        waves = jnp.concatenate(pieces[len(pieces) // 2 :], axis=1)
+        coef0[...] = jnp.concatenate([cosines[:, : half + 1], waves[:, 1:half]], axis=1)
         for q in range(lat_count * cap):
-            packed[l, q // cap, q % cap : q % cap + 1, :] = coef0[pl.ds(picks[q], 1), :][:, :nlon]
+            packed[l, q // cap, q % cap : q % cap + 1, :] = coef0[pl.ds(picks[q], 1), :]
         own_copy(l).start()
         for k in range(1, lat_count):
             spectra_copy(l, k).start()
-        for at in range(padded // CHUNK):
-            cols = slice(at * CHUNK, (at + 1) * CHUNK)
-            res[:, cols] = product(mid, high, at, True)
+        for side in range(2):
+            for at in range(padded // CHUNK):
+                res[side, :, at * CHUNK : (at + 1) * CHUNK] = product(mid, side, at, True)
         for f in range(fields):
             part = slice(f * rows_dev, (f + 1) * rows_dev)
-            out_buf[l, f] = out_buf[l, f] + jnp.where(flagged, res[part, :nlon], change[part, :])
+            even_part, odd_part = res[0, part, :half], res[1, part, :half]
+            filtered = jnp.concatenate([even_part + odd_part, even_part - odd_part], axis=1)
+            out_buf[l, f] = out_buf[l, f] + jnp.where(flagged, filtered, change[part, :])
         for copy in out_copies(l):
             copy.start()
         return carry
@@ -381,17 +414,16 @@
             copy.wait()
 
 
-def local(thickness, tracers, east, north, vert, flags, slots, high, low, rowc, sines):
+def local(thickness, tracers, east, north, vert, flags, slots, *tables):
     lat_count = lax.axis_size("lat")
     lev_count = lax.axis_size("lev")
     lev_dev, rows_dev, nlon = thickness.shape
-    padded = high.shape[0]
+    padded = tables[0].shape[1]
     fields = tracers.shape[0] + 1
     count = fields * rows_dev
     cap = -(-rows_dev // lat_count)
-    anywhere = pl.BlockSpec(memory_space=pl.ANY)
+    hbm = pl.BlockSpec(memory_space=pltpu.HBM)
     vmem = pl.BlockSpec(memory_space=pltpu.VMEM)
-    smem = pl.BlockSpec(memory_space=pltpu.SMEM)
     dma = pltpu.SemaphoreType.DMA
     return pl.pallas_call(
         functools.partial(kernel, lat_count, lev_count, cap),
@@ -400,31 +432,36 @@
             jax.ShapeDtypeStruct(tracers.shape, F32),
             jax.ShapeDtypeStruct((SLOT_DEV, lev_dev, nlon), F32),
         ),
-        in_specs=[anywhere] * 5 + [smem, smem, vmem] + [anywhere] * 3 + [vmem],
-        out_specs=(anywhere, anywhere, vmem),
+        in_specs=[hbm] * 13,
+        out_specs=(hbm, hbm, vmem),
         scratch_shapes=[
             pltpu.VMEM((4, rows_dev, nlon), F32),
             pltpu.VMEM((fields - 1, 4, rows_dev, nlon), F32),
             pltpu.VMEM((3, rows_dev, nlon), F32),
             pltpu.VMEM((2, rows_dev, nlon), F32),
             pltpu.VMEM((2, rows_dev, nlon), F32),
-            pltpu.VMEM((padded, padded), BF16),
-            pltpu.VMEM((padded, padded), BF16),
+            pltpu.VMEM((2, padded, padded), BF16),
+            pltpu.VMEM((2, padded, padded), BF16),
             pltpu.VMEM((rows_dev, 128), F32),
+            pltpu.VMEM((8, 2 * padded), F32),
+            pltpu.VMEM((CHUNK, CHUNK), BF16),
+            pltpu.VMEM((1, flags.shape[0]), jnp.int32),
+            pltpu.SMEM(flags.shape, jnp.int32),
+            pltpu.SMEM(flags.shape, jnp.int32),
             pltpu.VMEM((2, 16, nlon), F32),
             pltpu.VMEM((2, 16, nlon), F32),
             pltpu.VMEM((2, 16, nlon), F32),
             pltpu.VMEM((2, 16, nlon), F32),
-            pltpu.VMEM((rows_dev, padded), F32),
+            pltpu.VMEM((rows_dev, 2 * padded), F32),
             pltpu.VMEM((count, nlon), F32),
-            pltpu.VMEM((2 * count, padded), BF16),
-            pltpu.VMEM((2 * count, padded), BF16),
-            pltpu.VMEM((count, padded), F32),
-            pltpu.VMEM((rows_dev, padded), F32),
+            pltpu.VMEM((2, 2 * count, padded), BF16),
+            pltpu.VMEM((2, 2 * count, padded), BF16),
+            pltpu.VMEM((2, count, padded), F32),
+            pltpu.VMEM((rows_dev, nlon), F32),
             pltpu.VMEM((2, lat_count, cap, nlon), F32),
             pltpu.VMEM((2, lat_count, cap, nlon), F32),
             pltpu.VMEM((2, fields, rows_dev, nlon), F32),
-            dma((8,)),
+            dma((13,)),
             dma((5,)),
             dma((5,)),
             dma((2,)),
@@ -435,25 +472,24 @@
             dma((2, 2)),
         ],
         compiler_params=pltpu.CompilerParams(
-            collective_id=0, has_side_effects=True, vmem_limit_bytes=48 * 1024 * 1024
+            collective_id=0, has_side_effects=True, vmem_limit_bytes=56 * 1024 * 1024
         ),
-    )(thickness, tracers, east, north, vert, flags, slots, slots.reshape(1, -1), high, low, rowc, sines)
+    )(thickness, tracers, east, north, vert, flags, slots, slots.reshape(1, -1), *tables)
 
 
 def solution(mesh):
     def run(thickness, tracers, east, north, vert, flags, slots):
         total_rows, nlon = thickness.shape[1:]
-        padded = -(-nlon // CHUNK) * CHUNK
-        high, low = spectral_table(nlon, padded)
+        high, low = spectral_table(nlon)
         cells = P("lev", "lat", None)
         mapped = jax.shard_map(
             local,
             mesh=mesh,
-            in_specs=(cells, P(None, "lev", "lat", None), cells, cells, cells) + (P(),) * 6,
+            in_specs=(cells, P(None, "lev", "lat", None), cells, cells, cells) + (P(),) * 7,
             out_specs=(cells, P(None, "lev", "lat", None), P("lat", "lev", None)),
             check_vma=False,
         )
-        tables = (high, low, row_constants(total_rows), sine_rows(nlon, padded))
+        tables = (high, low, row_constants(total_rows), sine_rows(nlon), interleave())
         return mapped(
             thickness, tracers, east, north, vert, flags, slots, *(jnp.asarray(t) for t in tables)
         )

time: 42.7 us -> 34.3 us (0.80)
  local copies, waits for them, and re-layouts: 10.5 us -> 4.99 us
  Pallas kernels: 31.2 us -> 28.5 us
    unnamed x21 -> x5, local copies, waits for them, and re-layouts: 10.5 us -> 4.99 us
    pallas_call x1, Pallas kernels: 31.2 us -> 28.5 us  [local(): pl.pallas_call(functools.partial(kernel, lat_count, lev_count, cap), out_...]
where the time goes in v3:
time: 34.3 us; the launch traced here: 34.2 us
  Pallas kernels  28.5 us (83%)
  local copies, waits for them, and re-layouts  4.99 us (15%)
  between operations  0.64 us (2%)
    pallas_call x1, Pallas kernels, local(): pl.pallas_call(functools.partial(kernel, lat_count, lev_count, cap), out_...  28.5 us
    unnamed x5, local copies, waits for them, and re-layouts  4.99 us

profile of v3, /device:TPU:0, one launch (start us, length us, event | category | flops | bytes accessed | tf_op | source)
XLA Modules:
  0.0 34.2 jit_solution(5459511975530590830)
XLA Ops:
  0.6 28.5 %shard_map.139 = (f32[2,16,1440]{2,1,0:T(8,128)}, f32[8,2,16,1440]{3,2,1,0:T(8,128)}, f32[9,2,1440]{2,1,0:T(2,128)}) custom-call(f32[2,16,1440]{2,1,0:T(8,128)} %th_in.1, f32[8,2,16,1440]{3,2,1,0:T(8,128)} %tr_in.1, f32[2,16,1440]{2,1,0:T(8,128)} %east_in.1, f32[2,16,1440]{2,1,0:T(8,128)} %north_in.1, f32[2,16,1440]{2,1,0:T(8,128)} %vert_in.1, s32[128]{0:T(128)} %flags_in.1, ...), custom_call_target="tpu_custom_call" | custom-call | tf_op jit(solution)/shard_map/pallas_call | solution.py:428
  29.2 1.6 %copy.18 = f32[2,16,1440]{2,1,0:T(8,128)} copy(f32[2,16,1440]{2,1,0:T(8,128)} %get-tuple-element.6) | data formatting | bytes 368640
  30.8 0.0 copy-start
  30.8 2.7 %copy.19 = f32[8,2,16,1440]{3,2,1,0:T(8,128)} copy(f32[8,2,16,1440]{3,2,1,0:T(8,128)} %get-tuple-element.7) | data formatting | bytes 2949120
  33.5 0.0 copy-done
  33.5 0.6 %copy.20 = f32[9,2,1440]{2,1,0:T(2,128)} copy(f32[9,2,1440]{2,1,0:T(2,128)S(1)} %copy-done) | data formatting | bytes 207360
Async XLA Ops:
  30.8 2.7 %copy-start = (f32[9,2,1440]{2,1,0:T(2,128)S(1)}, f32[9,2,1440]{2,1,0:T(2,128)}, u32[]{:S(2)}) copy-start(f32[9,2,1440]{2,1,0:T(2,128)} %get-tuple-element.8) | copy-start | bytes 311044
